TPU v7x, 32 devices: a whole 2x2x4 slice. The times are simulated.
32 devices in a mesh: seq: 8 (over y, x, core), head: 4 (over z).
Axes of the slice: x: 2, y: 2, z: 4, core: 2. Of those that a mesh axis runs over, the one named last changes fastest.
Arguments:
- teacher_queries: bfloat16 [2048, 8192], P('seq', 'head'), may hold values from -16 to 16, as said below
- student_queries: bfloat16 [2048, 4096], P('seq', 'head'), may hold values from -16 to 16, as said below
- token_counts: int32 [8], replicated, may hold values from 1 to 256, 1536 in all
Outputs:
- student_grad: float32 [2048, 4096], P('seq', 'head')
- loss: float32 [], replicated
Inputs may be any that keep to these rules, and one draw needn't show every extreme that they name: `teacher_queries`: query entries are real values of order one; the entries of a row may share a scale. `student_queries`: query entries are real values of order one; the entries of a row may share a scale. `token_counts`: the counts sum to 1536; the largest equals 256.
All inputs are finite; a program needn't handle non-finite values.
Results may differ from a plain program's by a relative error of at most 0.0035.
Values may be sent and summed in bfloat16 or wider, within the bound.
No kernel may reach another device: no remote copies, remote signals or barrier semaphores. Data moves between devices by JAX's collectives and lax.ppermute only.
A program may use at most 64 MiB of HBM per device.

v0:
```python
import jax
import jax.numpy as jnp
from jax import lax
from jax.sharding import PartitionSpec as P

DT = 8192
DS = 4096
H_REL = 128


NEGATIVE = -1e30


def tile_logits(query_set, key_set, scales):
    teacher_logits = (
        jnp.einsum("rhd,khd->hrk", query_set[0], key_set[0], preferred_element_type=jnp.float32)
        * scales[0]
    )
    student_logits = (
        jnp.einsum("rhd,khd->hrk", query_set[1], key_set[1], preferred_element_type=jnp.float32)
        * scales[1]
    )
    row_pos = query_set[2]
    key_pos = key_set[2]
    allowed = (key_pos[None, :] <= row_pos[:, None]) & (
        key_set[3][None, :] | (key_pos[None, :] == row_pos[:, None])
    )
    return (teacher_logits, student_logits, allowed[None])


def grad_weights(query_set, stats, key_set, scales):
    teacher_logits, student_logits, allowed = tile_logits(query_set, key_set, scales)
    teacher_prob = (
        jnp.where(allowed, jnp.exp(teacher_logits - stats[0][..., None]), 0.0) / stats[1][..., None]
    )
    student_prob = (
        jnp.where(allowed, jnp.exp(student_logits - stats[2][..., None]), 0.0) / stats[3][..., None]
    )
    difference = jnp.where(query_set[3][None, :, None], student_prob - teacher_prob, 0.0)
    return difference.astype(jnp.bfloat16)


def row_statistics(query_set, halves, half_rows, select, scales):
    row_count = query_set[0].shape[0]
    heads_here = query_set[0].shape[1]
    lowest = jnp.full((heads_here, row_count), NEGATIVE, jnp.float32)
    zeros = jnp.zeros((heads_here, row_count), jnp.float32)

    def row_advance(index_now, loop_state):
        teacher_max, teacher_sum, cross_sum, student_max, student_sum = loop_state
        key_set = select(index_now * half_rows, half_rows)
        teacher_logits, student_logits, allowed = tile_logits(query_set, key_set, scales)
        teacher_top = jnp.maximum(
            teacher_max, jnp.max(jnp.where(allowed, teacher_logits, NEGATIVE), axis=2)
        )
        student_top = jnp.maximum(
            student_max, jnp.max(jnp.where(allowed, student_logits, NEGATIVE), axis=2)
        )
        teacher_weight = jnp.where(allowed, jnp.exp(teacher_logits - teacher_top[..., None]), 0.0)
        student_weight = jnp.where(allowed, jnp.exp(student_logits - student_top[..., None]), 0.0)
        teacher_shrink = jnp.exp(teacher_max - teacher_top)
        student_shrink = jnp.exp(student_max - student_top)
        teacher_sum = teacher_sum * teacher_shrink + jnp.sum(teacher_weight, axis=2)
        cross_sum = cross_sum * teacher_shrink + jnp.sum(
            teacher_weight * (teacher_logits - student_logits), axis=2
        )
        student_sum = student_sum * student_shrink + jnp.sum(student_weight, axis=2)
        return (teacher_top, teacher_sum, cross_sum, student_top, student_sum)

    teacher_max, teacher_sum, cross_sum, student_max, student_sum = lax.fori_loop(
        0, halves, row_advance, (lowest, zeros, zeros, lowest, zeros)
    )
    divergence = (
        cross_sum / teacher_sum
        - teacher_max
        - jnp.log(teacher_sum)
        + student_max
        + jnp.log(student_sum)
    )
    divergence_sum = jnp.sum(jnp.where(query_set[3][None, :], divergence, 0.0))
    return ((teacher_max, teacher_sum, student_max, student_sum), divergence_sum)


def spread_gradient(query_set, stats, halves, half_rows, select, scales, row_start, collected):
    query_grad = jnp.zeros(query_set[1].shape, jnp.float32)

    def spread_advance(index_now, loop_state):
        query_grad, collected = loop_state
        key_start = index_now * half_rows
        key_set = select(key_start, half_rows)
        weights = grad_weights(query_set, stats, key_set, scales)
        query_grad = query_grad + jnp.einsum(
            "hrk,khd->rhd", weights, key_set[1], preferred_element_type=jnp.float32
        )
        key_term = jnp.einsum(
            "hrk,rhd->khd", weights, query_set[1], preferred_element_type=jnp.float32
        )
        before = lax.dynamic_slice_in_dim(collected, key_start, half_rows, 0)
        collected = lax.dynamic_update_slice_in_dim(collected, before + key_term, key_start, 0)
        return (query_grad, collected)

    query_grad, collected = lax.fori_loop(0, halves, spread_advance, (query_grad, collected))
    before = lax.dynamic_slice_in_dim(collected, row_start, query_grad.shape[0], 0)
    return lax.dynamic_update_slice_in_dim(collected, before + query_grad, row_start, 0)


def local(teacher_queries, student_queries, token_counts):
    block_rows = teacher_queries.shape[0]
    half_rows = block_rows // 2
    heads_here = H_REL // lax.axis_size("head")
    teacher_dim = DT // H_REL
    student_dim = DS // H_REL
    scales = (teacher_dim ** (-0.5), student_dim ** (-0.5))
    blocks = lax.axis_size("seq")
    my_index = lax.axis_index("seq")
    seq_rows = block_rows * blocks
    teacher_all, student_all = (
        lax.all_gather(teacher_queries, "seq", axis=0, tiled=True),
        lax.all_gather(student_queries, "seq", axis=0, tiled=True),
    )
    teacher_all = teacher_all.reshape(seq_rows, heads_here, teacher_dim)
    student_all = student_all.reshape(seq_rows, heads_here, student_dim)
    positions = jnp.arange(seq_rows, dtype=jnp.int32)
    owner_table = (positions // block_rows)[:, None] == jnp.arange(blocks, dtype=jnp.int32)[None, :]
    real_count = jnp.sum(jnp.where(owner_table, token_counts[None, :], 0), axis=1)
    is_real = positions % block_rows < real_count

    def select(row_start, row_count):
        return (
            lax.dynamic_slice_in_dim(teacher_all, row_start, row_count, 0),
            lax.dynamic_slice_in_dim(student_all, row_start, row_count, 0),
            lax.dynamic_slice_in_dim(positions, row_start, row_count, 0),
            lax.dynamic_slice_in_dim(is_real, row_start, row_count, 0),
        )

    groups = [
        (my_index * half_rows, half_rows, my_index + 1),
        ((2 * blocks - 1 - my_index) * half_rows, half_rows, 2 * blocks - my_index),
    ]
    group_stats = []
    divergence_sum = jnp.zeros((), jnp.float32)
    for row_start, row_count, halves in groups:
        stats, group_sum = row_statistics(
            select(row_start, row_count), halves, half_rows, select, scales
        )
        group_stats.append(stats)
        divergence_sum = divergence_sum + group_sum
    loss = lax.psum(divergence_sum, ("seq", "head")) / (
        H_REL * jnp.sum(token_counts).astype(jnp.float32)
    )
    collected = jnp.zeros((seq_rows, heads_here, student_dim), jnp.float32)
    for (row_start, row_count, halves), stats in zip(groups, group_stats):
        collected = spread_gradient(
            select(row_start, row_count),
            stats,
            halves,
            half_rows,
            select,
            scales,
            row_start,
            collected,
        )
    terms = (collected * scales[1]).reshape(seq_rows, heads_here * student_dim)
    student_grad = lax.psum_scatter(terms, "seq", scatter_dimension=0, tiled=True)
    return (student_grad, loss)


def solution(mesh):
    return jax.shard_map(
        local,
        mesh=mesh,
        in_specs=(P("seq", "head"), P("seq", "head"), P()),
        out_specs=(P("seq", "head"), P()),
        check_vma=False,
    )
```

profile of v0, /device:TPU:0, one launch (start us, length us, event | category | flops | bytes accessed | tf_op | source)
XLA Modules:
  0.0 441.0 jit_solution(2998699810592260302)
XLA Ops:
  9.6 39.8 %all-gather.3.cloned.1.call-done = bf16[2048,1024]{1,0:T(8,128)(2,1)} async-done(((bf16[256,1024]{1,0:T(8,128)(2,1)}), bf16[2048,1024]{1,0:T(8,128)(2,1)}) %all-gather.3.cloned.1.call-update) | async-done | bytes 4194320 | tf_op jit(solution)/shard_map/all_gather | solution.py:119
  49.3 6.5 %copy.23 = bf16[2048,1024]{0,1:T(8,128)(2,1)} copy(bf16[2048,1024]{1,0:T(8,128)(2,1)} %all-gather.3.cloned.1.call-done) | data formatting | bytes 8388608 | tf_op jit(solution)/shard_map/all_gather | solution.py:119
  56.9 48.7 %all-gather.5.cloned.1.call-done = bf16[2048,2048]{1,0:T(8,128)(2,1)} async-done(((bf16[256,2048]{1,0:T(8,128)(2,1)}), bf16[2048,2048]{1,0:T(8,128)(2,1)}) %all-gather.5.cloned.1.call-update) | async-done | bytes 8388624 | tf_op jit(solution)/shard_map/all_gather | solution.py:118
  105.6 12.3 %copy.24 = bf16[2048,2048]{0,1:T(8,128)(2,1)} copy(bf16[2048,2048]{1,0:T(8,128)(2,1)} %all-gather.5.cloned.1.call-done) | data formatting | bytes 16777216 | tf_op jit(solution)/shard_map/all_gather | solution.py:118
  119.3 81.4 %while.62 = (s32[]{:T(128)}, f32[32,128]{1,0:T(8,128)S(1)}, f32[32,128]{1,0:T(8,128)S(1)}, f32[32,128]{1,0:T(8,128)S(1)}, f32[32,128]{1,0:T(8,128)S(1)}, /*index...) while((s32[]{:T(128)}, f32[32,128]{1,0:T(8,128)S(1)}, ...), condition=%wide.region_16.17_spmd, body=%wide.region_10.16_spmd.sunk | while | flops 109662216 | bytes 12601955 | solution.py:70
  200.8 5.1 %while.60 = (s32[]{:T(128)}, f32[32,128]{1,0:T(8,128)S(1)}, f32[32,128]{1,0:T(8,128)S(1)}, f32[32,128]{1,0:T(8,128)S(1)}, f32[32,128]{1,0:T(8,128)S(1)}, /*index...) while((s32[]{:T(128)}, f32[32,128]{1,0:T(8,128)S(1)}, ...), condition=%wide.region_7.8_spmd, body=%wide.region_1.7_spmd.sunk | while | flops 109662216 | bytes 12601955 | solution.py:70
  205.9 4.3 broadcast_in_dim.162
  210.2 8.0 %while.61 = (s32[]{:T(128)}, f32[128,32,32]{0,2,1:T(8,128)S(1)}, f32[2048,32,32]{0,2,1:T(8,128)}, s32[]{:T(128)}, bf16[2048,32,32]{0,2,1:T(8,128)(2,1)}, /*index...) while((s32[]{:T(128)}, f32[128,32,32]{0,2,1:T(8,128)S(1)}, ...), condition=%wide.region_9.10_spmd, body=%wide.region_8.9_spmd.sunk | while | flops 173867008 | bytes 11635451 | solution.py:102
  211.9 2.4 fusion.134
  214.3 2.5 fusion.136
  218.2 2.0 add_dynamic-update-slice_fusion.1
  220.2 127.9 %while.63 = (s32[]{:T(128)}, f32[128,32,32]{0,2,1:T(8,128)S(1)}, f32[2048,32,32]{0,2,1:T(8,128)}, s32[]{:T(128)}, bf16[2048,32,32]{0,2,1:T(8,128)(2,1)}, /*index...) while((s32[]{:T(128)}, f32[128,32,32]{0,2,1:T(8,128)S(1)}, ...), condition=%wide.region_18.19_spmd, body=%wide.region_17.18_spmd.sunk | while | flops 173867008 | bytes 11635451 | solution.py:102
  222.1 2.4 fusion.152
  224.5 2.5 fusion.154
  230.1 2.4 fusion.152
  232.5 2.6 fusion.154
  238.1 2.4 fusion.152
  240.5 2.6 fusion.154
  246.2 2.4 fusion.152
  248.5 2.5 fusion.154
  254.1 2.4 fusion.152
  256.5 2.6 fusion.154
  262.1 2.4 fusion.152
  264.5 2.5 fusion.154
  270.1 2.4 fusion.152
  272.4 2.5 fusion.154
  278.0 2.4 fusion.152
  280.4 2.6 fusion.154
  286.0 2.4 fusion.152
  288.4 2.5 fusion.154
  294.0 2.4 fusion.152
  296.4 2.5 fusion.154
  302.0 2.4 fusion.152
  304.3 2.6 fusion.154
  310.0 2.4 fusion.152
  312.3 2.6 fusion.154
  318.0 2.4 fusion.152
  320.3 2.6 fusion.154
  326.0 2.4 fusion.152
  328.3 2.5 fusion.154
  333.9 2.4 fusion.152
  336.3 2.5 fusion.154
  341.9 2.4 fusion.152
  344.3 2.5 fusion.154
  350.1 8.4 %broadcast_multiply_fusion = f32[2048,32,32]{0,2,1:T(8,128)} fusion(f32[2048,32,32]{0,2,1:T(8,128)} %add_dynamic-update-slice_fusion), kind=kLoop, calls=%fused_computation.92 | loop fusion | flops 2097152 | bytes 16777216 | tf_op jit(solution)/shard_map/mul | solution.py:163
  362.4 39.6 %psum.7 = f32[]{:T(128)} all-reduce(f32[]{:T(128)S(6)} %add.143), channel_id=1, replica_groups=mesh['seq'=8,'head'=4] {'seq','head'}, use_global_device_ids=true, to_apply=%region_22.23 | all-reduce | flops 1 | bytes 8 | tf_op jit(solution)/shard_map/psum | solution.py:148
  402.7 28.1 %reduce-scatter.2.cloned.1.call-done = f32[256,1024]{0,1:T(8,128)} async-done(((f32[2048,1024]{0,1:T(8,128)}), f32[256,1024]{0,1:T(8,128)}) %reduce-scatter.2.cloned.1.call-update) | async-done | bytes 1048592 | tf_op jit(solution)/shard_map/reduce_scatter | solution.py:164
  430.8 2.5 copy.25
  (307 shorter events, 145.5 us)
Async XLA Ops:
  7.2 42.2 %all-gather.3.cloned.1.call-start = ((), (), s32[]{:S(2)}) async-start(), calls=%async_computation.1 | async-start | bytes 4718592 | tf_op jit(solution)/shard_map/all_gather | solution.py:119
  7.9 97.7 %all-gather.5.cloned.1.call-start = ((), (), s32[]{:S(2)}) async-start(), calls=%async_computation.2 | async-start | bytes 9437184 | tf_op jit(solution)/shard_map/all_gather | solution.py:118
  8.6 422.2 %reduce-scatter.2.cloned.1.call-start = ((), (), s32[]{:S(2)}) async-start(), calls=%async_computation.3 | async-start | bytes 9437184 | tf_op jit(solution)/shard_map/reduce_scatter | solution.py:164
  358.6 0.7 copy-start
Sparse Core Ops, SparseCore 0:
  9.9 39.4 all-gather.2
  51.2 54.3 all-gather.4
  358.7 72.0 reduce-scatter.1
where the time goes:
time: 446 us; the launch traced here: 441 us
  matrix products  186 us (42%)
  waiting for transfers between devices  118 us (26%)
  other arithmetic  42.9 us (10%)
  blocking collectives  39.6 us (9%)
  local copies, waits for them, and re-layouts  34.2 us (8%)
  between operations  17.7 us (4%)
    dot_general x34, matrix products, tile_logits(): jnp.einsum('rhd,khd->hrk', query_set[0], key_set[0], preferred_element_ty...  66.2 us
    dot_general x34, matrix products, tile_logits(): jnp.einsum('rhd,khd->hrk', query_set[1], key_set[1], preferred_element_ty...  54 us
    all_gather x1, waiting for transfers between devices, local(): lax.all_gather(teacher_queries, 'seq', axis=0, tiled=True)  48.7 us
    dot_general x17, matrix products, spread_advance(): jnp.einsum('hrk,rhd->khd', weights, query_set[1], preferred_element_type=...  43.4 us
    all_gather x1, waiting for transfers between devices, local(): lax.all_gather(student_queries, 'seq', axis=0, tiled=True)  39.8 us
    psum x1, blocking collectives, local(): lax.psum(divergence_sum, ('seq', 'head'))  39.6 us
    reduce_scatter x1, waiting for transfers between devices, local(): lax.psum_scatter(terms, 'seq', scatter_dimension=0, tiled=True)  28.1 us
    reduce_sum x17, other arithmetic, row_advance(): jnp.sum(teacher_weight * (teacher_logits - student_logits), axis=2)  24.4 us
  transfers between devices with their start and end apart: 3, of which 3 were waited for; matrix products, arithmetic and copies ran while one was open for 2% of the time, Pallas kernels for 0%

commit v1 on v0

v1 whole, which is shorter than its diff:
```python
import functools
import math

import jax
import jax.numpy as jnp
from jax import lax
from jax.experimental import pallas as pl
from jax.experimental.pallas import tpu as pltpu
from jax.sharding import PartitionSpec as P

DT = 8192
DS = 4096
H_REL = 128
TEACHER_DIM = DT // H_REL
STUDENT_DIM = DS // H_REL

NEGATIVE = -1e30
LOG2E = math.log2(math.e)
PAD = 8


def split_high_low(values):
    high = values.astype(jnp.bfloat16)
    low = (values - high.astype(jnp.float32)).astype(jnp.bfloat16)
    return high, low


def relation_kernel(
    blocks,
    heads,
    tiles,
    counts_ref,
    teacher_ref,
    student_ref,
    grad_ref,
    kl_ref,
    teacher_pack,
    student_pack,
    teacher_key,
    student_key,
    teacher_row,
    student_row,
    student_col,
    teacher_prob,
    student_prob,
    grad_cols,
    grad_rows,
):
    rows = teacher_ref.shape[0] // blocks
    live = tiles * rows

    offsets = []
    start = 0
    for b in range(blocks):
        offsets.append(start)
        start = start + counts_ref[b]

    window = rows + PAD
    position = lax.broadcasted_iota(jnp.int32, (window, rows), 0)
    token = lax.broadcasted_iota(jnp.int32, (window, rows), 1)
    teacher_pack[pl.ds(0, PAD), :] = jnp.zeros((PAD, teacher_pack.shape[1]), jnp.float32)
    student_pack[pl.ds(0, PAD), :] = jnp.zeros((PAD, student_pack.shape[1]), jnp.float32)
    bases, shifts = [], []
    for b in range(blocks):
        here = pl.ds(b * rows, rows)
        base = pl.multiple_of(offsets[b] // PAD * PAD, PAD) if b else 0
        shift = offsets[b] - base
        bases.append(base)
        shifts.append(shift)
        place = ((position == token + shift) & (token < counts_ref[b])).astype(jnp.bfloat16)
        for source, pack in ((teacher_ref, teacher_pack), (student_ref, student_pack)):
            moved = jnp.dot(place, source[here, :], preferred_element_type=jnp.float32)
            pack[pl.ds(base, PAD), :] = pack[pl.ds(base, PAD), :] + moved[:PAD]
            pack[pl.ds(base + PAD, rows), :] = moved[PAD:]

    for h in range(heads):
        for i in range(tiles):
            here = pl.ds(i * rows, rows)
            teacher = teacher_pack[here, h * TEACHER_DIM : (h + 1) * TEACHER_DIM]
            student = student_pack[here, h * STUDENT_DIM : (h + 1) * STUDENT_DIM]
            tb = teacher.astype(jnp.bfloat16)
            sb = student.astype(jnp.bfloat16)
            teacher_key[h, here, :] = jnp.concatenate([tb, tb], axis=1)
            student_key[h, here, :] = jnp.concatenate([sb, sb], axis=1)
            teacher_t = teacher.T
            student_t = student.T
            high, low = split_high_low(teacher_t * (LOG2E * TEACHER_DIM**-0.5))
            teacher_row[h, i] = jnp.concatenate([high, low], axis=0)
            high, low = split_high_low(student_t * (LOG2E * STUDENT_DIM**-0.5))
            student_row[h, i] = jnp.concatenate([high, low], axis=0)
            student_col[h, i] = student_t.astype(jnp.bfloat16)

    diag_allowed = lax.broadcasted_iota(jnp.int32, (rows, rows), 0) <= lax.broadcasted_iota(
        jnp.int32, (rows, rows), 1
    )

    def head_step(h, kl_total):
        for i in range(tiles):
            stats = []
            for j in range(i + 1):
                keys = pl.ds(j * rows, rows)
                teacher = jnp.dot(
                    teacher_key[h, keys, :], teacher_row[h, i], preferred_element_type=jnp.float32
                )
                student = jnp.dot(
                    student_key[h, keys, :], student_row[h, i], preferred_element_type=jnp.float32
                )
                if i == j:
                    teacher = jnp.where(diag_allowed, teacher, NEGATIVE)
                    student = jnp.where(diag_allowed, student, NEGATIVE)
                teacher_top = jnp.max(teacher, axis=0, keepdims=True)
                student_top = jnp.max(student, axis=0, keepdims=True)
                teacher_exp = jnp.exp2(teacher - teacher_top)
                student_exp = jnp.exp2(student - student_top)
                teacher_prob[j] = teacher_exp
                student_prob[j] = student_exp
                stats.append(
                    (
                        teacher_top,
                        student_top,
                        jnp.sum(teacher_exp, axis=0, keepdims=True),
                        jnp.sum(student_exp, axis=0, keepdims=True),
                        jnp.sum(teacher_exp * (teacher - student), axis=0, keepdims=True),
                    )
                )
            teacher_max = functools.reduce(jnp.maximum, [s[0] for s in stats])
            student_max = functools.reduce(jnp.maximum, [s[1] for s in stats])
            teacher_fix = [jnp.exp2(s[0] - teacher_max) for s in stats]
            student_fix = [jnp.exp2(s[1] - student_max) for s in stats]
            teacher_sum = sum(f * s[2] for f, s in zip(teacher_fix, stats))
            student_sum = sum(f * s[3] for f, s in zip(student_fix, stats))
            cross_sum = sum(f * s[4] for f, s in zip(teacher_fix, stats))
            divergence = (
                cross_sum / teacher_sum
                - teacher_max
                - jnp.log2(teacher_sum)
                + student_max
                + jnp.log2(student_sum)
            )
            kl_total = kl_total + divergence
            teacher_inv = 1.0 / teacher_sum
            student_inv = 1.0 / student_sum
            row_grad = jnp.zeros((STUDENT_DIM, rows), jnp.float32)
            for j in range(i + 1):
                weights = (
                    student_prob[j] * (student_fix[j] * student_inv)
                    - teacher_prob[j] * (teacher_fix[j] * teacher_inv)
                ).astype(jnp.bfloat16)
                row_grad = row_grad + jnp.dot(
                    student_col[h, j], weights, preferred_element_type=jnp.float32
                )
                key_grad = lax.dot_general(
                    student_col[h, i],
                    weights,
                    (((1,), (1,)), ((), ())),
                    preferred_element_type=jnp.float32,
                )
                if j < i:
                    grad_cols[h, j] = grad_cols[h, j] + key_grad
                else:
                    grad_cols[h, i] = row_grad + key_grad
        return kl_total

    kl_total = lax.fori_loop(0, heads, head_step, jnp.zeros((1, rows), jnp.float32))
    kl_ref[...] = kl_total * math.log(2.0)

    for i in range(tiles):
        columns = grad_cols[:, i].reshape(heads * STUDENT_DIM, rows)
        grad_rows[pl.ds(i * rows, rows), :] = columns.T * (STUDENT_DIM**-0.5)
    grad_rows[pl.ds(live, window), :] = jnp.zeros((window, heads * STUDENT_DIM), jnp.float32)
    position = lax.broadcasted_iota(jnp.int32, (rows, window), 1)
    token = lax.broadcasted_iota(jnp.int32, (rows, window), 0)
    for b in range(blocks):
        place = ((position == token + shifts[b]) & (token < counts_ref[b])).astype(jnp.bfloat16)
        block = grad_rows[pl.ds(bases[b], window), :].astype(jnp.bfloat16)
        grad_ref[pl.ds(b * rows, rows), :] = jnp.dot(
            place, block, preferred_element_type=jnp.float32
        ).astype(grad_ref.dtype)


def relation(teacher, student, token_counts):
    blocks = token_counts.shape[0]
    tokens = teacher.shape[0]
    rows = tokens // blocks
    tiles = tokens * 3 // 4 // rows
    heads = teacher.shape[1] // TEACHER_DIM
    live = tiles * rows
    f32, bf16 = jnp.float32, jnp.bfloat16
    vmem = pl.BlockSpec(memory_space=pltpu.VMEM)
    return pl.pallas_call(
        functools.partial(relation_kernel, blocks, heads, tiles),
        in_specs=[pl.BlockSpec(memory_space=pltpu.SMEM), vmem, vmem],
        out_specs=[vmem, vmem],
        out_shape=[
            jax.ShapeDtypeStruct((tokens, heads * STUDENT_DIM), bf16),
            jax.ShapeDtypeStruct((1, rows), f32),
        ],
        scratch_shapes=[
            pltpu.VMEM((live + rows + PAD, heads * TEACHER_DIM), f32),
            pltpu.VMEM((live + rows + PAD, heads * STUDENT_DIM), f32),
            pltpu.VMEM((heads, live, 2 * TEACHER_DIM), bf16),
            pltpu.VMEM((heads, live, 2 * STUDENT_DIM), bf16),
            pltpu.VMEM((heads, tiles, 2 * TEACHER_DIM, rows), bf16),
            pltpu.VMEM((heads, tiles, 2 * STUDENT_DIM, rows), bf16),
            pltpu.VMEM((heads, tiles, STUDENT_DIM, rows), bf16),
            pltpu.VMEM((tiles, rows, rows), f32),
            pltpu.VMEM((tiles, rows, rows), f32),
            pltpu.VMEM((heads, tiles, STUDENT_DIM, rows), f32),
            pltpu.VMEM((live + rows + PAD, heads * STUDENT_DIM), f32),
        ],
        compiler_params=pltpu.CompilerParams(vmem_limit_bytes=48 * 1024 * 1024),
        name="relation",
    )(token_counts, teacher, student)


def local(teacher_queries, student_queries, token_counts):
    teacher = lax.all_to_all(teacher_queries, "seq", 1, 0, tiled=True)
    student = lax.all_to_all(student_queries, "seq", 1, 0, tiled=True)
    grad, kl = relation(teacher, student, token_counts)
    loss = lax.psum(jnp.sum(kl), ("seq", "head")) / (
        H_REL * jnp.sum(token_counts).astype(jnp.float32)
    )
    student_grad = lax.all_to_all(grad, "seq", 0, 1, tiled=True).astype(jnp.float32)
    return (student_grad, loss)


def solution(mesh):
    return jax.shard_map(
        local,
        mesh=mesh,
        in_specs=(P("seq", "head"), P("seq", "head"), P()),
        out_specs=(P("seq", "head"), P()),
        check_vma=False,
    )
```

time: 446 us -> 113 us (0.25); the launches traced: 441 us -> 113 us
  matrix products: 186 us -> 0 us
  waiting for transfers between devices: 118 us -> 9.66 us
  other arithmetic: 42.9 us -> 2.33 us
  local copies, waits for them, and re-layouts: 34.2 us -> 2.65 us
  Pallas kernels: 0 us -> 27.3 us
  blocking collectives: 39.6 us -> 59 us
  between operations: 17.7 us -> 3.12 us
  starting transfers between devices: 0.11 us -> 8.66 us
    dot_general x102 -> x0, matrix products: 186 us -> none  [the longest x34 66.2 us: tile_logits(): jnp.einsum('rhd,khd->hrk', query_set[0], key_set[0], preferred_element_ty...]
    all_gather x2 -> x0, waiting for transfers between devices: 88.5 us -> none  [the longest x1 48.7 us: local(): lax.all_gather(teacher_queries, 'seq', axis=0, tiled=True)]
    reduce_scatter x1 -> x0, waiting for transfers between devices: 28.1 us -> none  [local(): lax.psum_scatter(terms, 'seq', scatter_dimension=0, tiled=True)]
    pallas_call x0 -> x1, Pallas kernels: none -> 27.3 us  [relation(): pl.pallas_call(functools.partial(relation_kernel, blocks, heads, tiles),...]
    reduce_sum x19 -> x1, other arithmetic: 25.8 us -> 0.6 us  [local(): jnp.sum(kl)]
    all_gather x2 -> x0, local copies, waits for them, and re-layouts: 18.8 us -> none  [the longest x1 12.3 us: local(): lax.all_gather(teacher_queries, 'seq', axis=0, tiled=True)]
    all_to_all x0 -> x1, blocking collectives: none -> 17.8 us  [local(): teacher = lax.all_to_all(teacher_queries, 'seq', 1, 0, tiled=True)]
    all_to_all x0 -> x2, waiting for transfers between devices: none -> 9.66 us  [the longest x1 9.66 us: local(): student = lax.all_to_all(student_queries, 'seq', 1, 0, tiled=True)]
  transfers between devices with their start and end apart: 3 -> 2, of which waited for: 3 -> 1; matrix products, arithmetic and copies ran while one was open for 2% -> 1% of each run, Pallas kernels for 0% -> 0%
where the time goes in v1:
time: 113 us
  blocking collectives  59 us (52%)
  Pallas kernels  27.3 us (24%)
  waiting for transfers between devices  9.66 us (9%)
  starting transfers between devices  8.66 us (8%)
  between operations  3.12 us (3%)
  local copies, waits for them, and re-layouts  2.65 us (2%)
  other arithmetic  2.33 us (2%)
    psum x1, blocking collectives, local(): lax.psum(jnp.sum(kl), ('seq', 'head'))  41.2 us
    pallas_call x1, Pallas kernels, relation(): pl.pallas_call(functools.partial(relation_kernel, blocks, heads, tiles),...  27.3 us
    all_to_all x1, blocking collectives, local(): teacher = lax.all_to_all(teacher_queries, 'seq', 1, 0, tiled=True)  17.8 us
    all_to_all x1, waiting for transfers between devices, local(): student = lax.all_to_all(student_queries, 'seq', 1, 0, tiled=True)  9.66 us
    all_to_all x1, starting transfers between devices, local(): student = lax.all_to_all(student_queries, 'seq', 1, 0, tiled=True)  5.17 us
    all_to_all x1, starting transfers between devices, local(): lax.all_to_all(grad, 'seq', 0, 1, tiled=True).astype(jnp.float32)  3.49 us
  transfers between devices with their start and end apart: 2, of which 1 were waited for; matrix products, arithmetic and copies ran while one was open for 1% of the time, Pallas kernels for 0%

profile of v1, /device:TPU:0, one launch (start us, length us, event | category | flops | bytes accessed | tf_op | source)
XLA Modules:
  0.0 112.7 jit_solution(8176730572324493429)
XLA Ops:
  0.6 0.0 copy-start
  0.6 0.0 copy-start.2
  0.7 1.0 copy-done
  1.7 0.9 copy_bitcast_fusion.2
  2.6 5.2 %all-to-all-start.1 = ((bf16[256,8,128]{2,0,1:T(8,128)(2,1)}), bf16[256,8,128]{2,0,1:T(8,128)(2,1)S(1)}, u32[]{:S(2)}, u32[]{:S(2)}) async-start(bf16[256,8,128]{2,0,1:T(8,128)(2,1)} %copy_bitcast_fusion.2), calls=%async_computation.1 | async-start | bytes 1048576 | tf_op jit(solution)/shard_map/all_to_all | solution.py:218
  7.7 0.0 copy-done.2
  7.7 0.1 copy.14
  7.8 9.7 %all-to-all-done.1 = bf16[256,8,128]{2,0,1:T(8,128)(2,1)S(1)} async-done(((bf16[256,8,128]{2,0,1:T(8,128)(2,1)}), bf16[256,8,128]{2,0,1:T(8,128)(2,1)S(1)}, u32[]{:S(2)}, u32[]{:S(2)}) %all-to-all-start.1) | async-done | bytes 524320 | tf_op jit(solution)/shard_map/all_to_all | solution.py:218
  17.5 17.8 %all_to_all.51 = bf16[256,8,256]{2,0,1:T(8,128)(2,1)S(1)} all-to-all(bf16[256,8,256]{2,0,1:T(8,128)(2,1)S(1)} %bitcast.24), channel_id=1, replica_groups=mesh['seq'=8,'head'=4] {'seq'}, dimensions={1} | all-to-all | bytes 2097152 | tf_op jit(solution)/shard_map/all_to_all | solution.py:217
  35.3 0.0 copy-start.1
  35.3 0.7 copy-done.1
  35.9 27.3 %relation.1 = (bf16[2048,128]{1,0:T(8,128)(2,1)}, f32[1,256]{1,0:T(1,128)S(1)}) custom-call(s32[8]{0:T(128)S(1)} %copy-done.1, bf16[2048,256]{1,0:T(8,128)(2,1)S(1)} %bitcast.22, bf16[2048,128]{1,0:T(8,128)(2,1)S(1)} %bitcast.23), custom_call_target="tpu_custom_call" | custom-call | tf_op jit(solution)/shard_map/relation/pallas_call | solution.py:190
  63.2 3.5 %all-to-all-start.2 = ((bf16[8,256,128]{2,1,0:T(8,128)(2,1)}), bf16[8,256,128]{2,1,0:T(8,128)(2,1)S(1)}, u32[]{:S(2)}, u32[]{:S(2)}) async-start(bf16[8,256,128]{2,1,0:T(8,128)(2,1)} %bitcast.4), calls=%async_computation.2 | async-start | bytes 1048576 | tf_op jit(solution)/shard_map/all_to_all | solution.py:223
  66.7 0.6 reduce_sum.19
  68.0 0.6 reduce_sum.18
  68.6 41.2 %psum.7 = f32[]{:T(128)} all-reduce(f32[]{:T(128)} %reduce_sum.18), channel_id=1, replica_groups=mesh['seq'=8,'head'=4] {'seq','head'}, use_global_device_ids=true, to_apply=%region_1.0 | all-reduce | flops 1 | bytes 8 | tf_op jit(solution)/shard_map/psum | solution.py:220
  110.4 0.0 all-to-all-done.2
  110.4 1.1 copy_bitcast_fusion
Async XLA Ops:
  0.6 1.0 copy-start
  0.6 7.1 %copy-start.2 = (bf16[256,2048]{1,0:T(8,128)(2,1)S(1)}, bf16[256,2048]{1,0:T(8,128)(2,1)}, u32[]{:S(2)}) copy-start(bf16[256,2048]{1,0:T(8,128)(2,1)} %param.3) | copy-start | bytes 3145732
  2.6 14.9 %all-to-all-start.1 = ((bf16[256,8,128]{2,0,1:T(8,128)(2,1)}), bf16[256,8,128]{2,0,1:T(8,128)(2,1)S(1)}, u32[]{:S(2)}, u32[]{:S(2)}) async-start(bf16[256,8,128]{2,0,1:T(8,128)(2,1)} %copy_bitcast_fusion.2), calls=%async_computation.1 | async-start | bytes 1048576 | tf_op jit(solution)/shard_map/all_to_all | solution.py:218
  35.3 0.7 copy-start.1
  63.2 47.2 %all-to-all-start.2 = ((bf16[8,256,128]{2,1,0:T(8,128)(2,1)}), bf16[8,256,128]{2,1,0:T(8,128)(2,1)S(1)}, u32[]{:S(2)}, u32[]{:S(2)}) async-start(bf16[8,256,128]{2,1,0:T(8,128)(2,1)} %bitcast.4), calls=%async_computation.2 | async-start | bytes 1048576 | tf_op jit(solution)/shard_map/all_to_all | solution.py:223

commit v2 on v1

--- a/solution.py
+++ b/solution.py
@@ -17,6 +17,7 @@
 NEGATIVE = -1e30
 LOG2E = math.log2(math.e)
 PAD = 8
+LANES = 128
 
 
 def split_high_low(values):
@@ -25,59 +26,82 @@
     return high, low
 
 
-def relation_kernel(
-    blocks,
-    heads,
-    tiles,
-    counts_ref,
-    teacher_ref,
-    student_ref,
-    grad_ref,
-    kl_ref,
-    teacher_pack,
-    student_pack,
-    teacher_key,
-    student_key,
-    teacher_row,
-    student_row,
-    student_col,
-    teacher_prob,
-    student_prob,
-    grad_cols,
-    grad_rows,
-):
-    rows = teacher_ref.shape[0] // blocks
+def at_columns(index, count, width, act):
+    if width % LANES == 0:
+        act(pl.ds(pl.multiple_of(index * width, LANES), width))
+    else:
+        for part in range(count):
+            pl.when(index == part)(functools.partial(act, pl.ds(part * width, width)))
+
+
+def pack_kernel(blocks, me_ref, teacher_ref, student_ref, *sends):
+    teacher_width = teacher_ref.shape[1] // blocks
+    student_width = student_ref.shape[1] // blocks
+    for k in range(blocks):
+        to = jnp.bitwise_xor(me_ref[0], k)
+
+        def put_teacher(columns, send=sends[k]):
+            send[:, :teacher_width] = teacher_ref[:, columns]
+
+        def put_student(columns, send=sends[k]):
+            send[:, teacher_width:] = student_ref[:, columns]
+
+        at_columns(to, blocks, teacher_width, put_teacher)
+        at_columns(to, blocks, student_width, put_student)
+
+
+def unpack_kernel(blocks, live, me_ref, kl_ref, *refs):
+    grad_ref, loss_ref = refs[blocks:]
+    for k in range(blocks):
+
+        def put(columns, source=refs[k]):
+            grad_ref[:, columns] = source[...].astype(jnp.float32)
+
+        at_columns(jnp.bitwise_xor(me_ref[0], k), blocks, refs[k].shape[1], put)
+    total = jnp.sum(kl_ref[...], axis=0, keepdims=True)
+    loss_ref[...] = total * (1.0 / (H_REL * live))
+
+
+def relation_kernel(blocks, heads, tiles, me_ref, counts_ref, *refs):
+    sources = refs[:blocks]
+    grads = refs[blocks : 2 * blocks]
+    (
+        kl_ref,
+        pack,
+        teacher_key,
+        student_key,
+        teacher_row,
+        student_row,
+        student_col,
+        teacher_prob,
+        student_prob,
+        grad_cols,
+        grad_rows,
+    ) = refs[2 * blocks :]
+    rows = sources[0].shape[0]
     live = tiles * rows
-
-    offsets = []
-    start = 0
-    for b in range(blocks):
-        offsets.append(start)
-        start = start + counts_ref[b]
-
     window = rows + PAD
+    student_at = heads * TEACHER_DIM
+
     position = lax.broadcasted_iota(jnp.int32, (window, rows), 0)
     token = lax.broadcasted_iota(jnp.int32, (window, rows), 1)
-    teacher_pack[pl.ds(0, PAD), :] = jnp.zeros((PAD, teacher_pack.shape[1]), jnp.float32)
-    student_pack[pl.ds(0, PAD), :] = jnp.zeros((PAD, student_pack.shape[1]), jnp.float32)
-    bases, shifts = [], []
-    for b in range(blocks):
-        here = pl.ds(b * rows, rows)
-        base = pl.multiple_of(offsets[b] // PAD * PAD, PAD) if b else 0
-        shift = offsets[b] - base
-        bases.append(base)
-        shifts.append(shift)
-        place = ((position == token + shift) & (token < counts_ref[b])).astype(jnp.bfloat16)
-        for source, pack in ((teacher_ref, teacher_pack), (student_ref, student_pack)):
-            moved = jnp.dot(place, source[here, :], preferred_element_type=jnp.float32)
-            pack[pl.ds(base, PAD), :] = pack[pl.ds(base, PAD), :] + moved[:PAD]
-            pack[pl.ds(base + PAD, rows), :] = moved[PAD:]
+    pack[...] = jnp.zeros(pack.shape, jnp.float32)
+    places = []
+    for k in range(blocks):
+        owner = jnp.bitwise_xor(me_ref[0], k)
+        start = sum(jnp.where(b < owner, counts_ref[b], 0) for b in range(blocks))
+        base = pl.multiple_of(start // PAD * PAD, PAD)
+        places.append((base, start - base, counts_ref[owner]))
+    for source, (base, shift, count) in zip(sources, places):
+        place = ((position == token + shift) & (token < count)).astype(jnp.bfloat16)
+        moved = jnp.dot(place, source[...], preferred_element_type=jnp.float32)
+        pack[pl.ds(base, window), :] = pack[pl.ds(base, window), :] + moved
 
     for h in range(heads):
         for i in range(tiles):
             here = pl.ds(i * rows, rows)
-            teacher = teacher_pack[here, h * TEACHER_DIM : (h + 1) * TEACHER_DIM]
-            student = student_pack[here, h * STUDENT_DIM : (h + 1) * STUDENT_DIM]
+            teacher = pack[here, h * TEACHER_DIM : (h + 1) * TEACHER_DIM]
+            student = pack[here, student_at + h * STUDENT_DIM : student_at + (h + 1) * STUDENT_DIM]
             tb = teacher.astype(jnp.bfloat16)
             sb = student.astype(jnp.bfloat16)
             teacher_key[h, here, :] = jnp.concatenate([tb, tb], axis=1)
@@ -162,7 +186,9 @@
         return kl_total
 
     kl_total = lax.fori_loop(0, heads, head_step, jnp.zeros((1, rows), jnp.float32))
-    kl_ref[...] = kl_total * math.log(2.0)
+    kl_ref[...] = jnp.broadcast_to(
+        jnp.sum(kl_total, axis=1, keepdims=True) * math.log(2.0), kl_ref.shape
+    )
 
     for i in range(tiles):
         columns = grad_cols[:, i].reshape(heads * STUDENT_DIM, rows)
@@ -170,34 +196,49 @@
     grad_rows[pl.ds(live, window), :] = jnp.zeros((window, heads * STUDENT_DIM), jnp.float32)
     position = lax.broadcasted_iota(jnp.int32, (rows, window), 1)
     token = lax.broadcasted_iota(jnp.int32, (rows, window), 0)
-    for b in range(blocks):
-        place = ((position == token + shifts[b]) & (token < counts_ref[b])).astype(jnp.bfloat16)
-        block = grad_rows[pl.ds(bases[b], window), :].astype(jnp.bfloat16)
-        grad_ref[pl.ds(b * rows, rows), :] = jnp.dot(
-            place, block, preferred_element_type=jnp.float32
-        ).astype(grad_ref.dtype)
-
-
-def relation(teacher, student, token_counts):
-    blocks = token_counts.shape[0]
-    tokens = teacher.shape[0]
-    rows = tokens // blocks
-    tiles = tokens * 3 // 4 // rows
-    heads = teacher.shape[1] // TEACHER_DIM
+    for grad, (base, shift, count) in zip(grads, places):
+        place = ((position == token + shift) & (token < count)).astype(jnp.bfloat16)
+        block = grad_rows[pl.ds(base, window), :].astype(jnp.bfloat16)
+        grad[...] = jnp.dot(place, block, preferred_element_type=jnp.float32).astype(grad.dtype)
+
+
+def local(teacher_queries, student_queries, token_counts):
+    f32, bf16 = jnp.float32, jnp.bfloat16
+    blocks = lax.axis_size("seq")
+    devices = blocks * lax.axis_size("head")
+    rows = teacher_queries.shape[0]
+    heads = teacher_queries.shape[1] // TEACHER_DIM // blocks
+    tiles = blocks * 3 // 4
     live = tiles * rows
-    f32, bf16 = jnp.float32, jnp.bfloat16
+    width = heads * (TEACHER_DIM + STUDENT_DIM)
     vmem = pl.BlockSpec(memory_space=pltpu.VMEM)
-    return pl.pallas_call(
+    smem = pl.BlockSpec(memory_space=pltpu.SMEM)
+    params = pltpu.CompilerParams(vmem_limit_bytes=48 * 1024 * 1024)
+    me = lax.axis_index("seq").reshape(1)
+
+    def exchange(sends):
+        return [
+            send if k == 0 else lax.ppermute(send, "seq", [(i, i ^ k) for i in range(blocks)])
+            for k, send in enumerate(sends)
+        ]
+
+    sends = pl.pallas_call(
+        functools.partial(pack_kernel, blocks),
+        in_specs=[smem, vmem, vmem],
+        out_specs=[vmem] * blocks,
+        out_shape=[jax.ShapeDtypeStruct((rows, width), bf16)] * blocks,
+        compiler_params=params,
+        name="pack",
+    )(me, teacher_queries, student_queries)
+    sources = exchange(sends)
+    *grads, kl = pl.pallas_call(
         functools.partial(relation_kernel, blocks, heads, tiles),
-        in_specs=[pl.BlockSpec(memory_space=pltpu.SMEM), vmem, vmem],
-        out_specs=[vmem, vmem],
-        out_shape=[
-            jax.ShapeDtypeStruct((tokens, heads * STUDENT_DIM), bf16),
-            jax.ShapeDtypeStruct((1, rows), f32),
-        ],
+        in_specs=[smem, smem] + [vmem] * blocks,
+        out_specs=[vmem] * (blocks + 1),
+        out_shape=[jax.ShapeDtypeStruct((rows, heads * STUDENT_DIM), bf16)] * blocks
+        + [jax.ShapeDtypeStruct((devices, 128), f32)],
         scratch_shapes=[
-            pltpu.VMEM((live + rows + PAD, heads * TEACHER_DIM), f32),
-            pltpu.VMEM((live + rows + PAD, heads * STUDENT_DIM), f32),
+            pltpu.VMEM((live + rows + PAD, width), f32),
             pltpu.VMEM((heads, live, 2 * TEACHER_DIM), bf16),
             pltpu.VMEM((heads, live, 2 * STUDENT_DIM), bf16),
             pltpu.VMEM((heads, tiles, 2 * TEACHER_DIM, rows), bf16),
@@ -208,20 +249,23 @@
             pltpu.VMEM((heads, tiles, STUDENT_DIM, rows), f32),
             pltpu.VMEM((live + rows + PAD, heads * STUDENT_DIM), f32),
         ],
-        compiler_params=pltpu.CompilerParams(vmem_limit_bytes=48 * 1024 * 1024),
+        compiler_params=params,
         name="relation",
-    )(token_counts, teacher, student)
-
-
-def local(teacher_queries, student_queries, token_counts):
-    teacher = lax.all_to_all(teacher_queries, "seq", 1, 0, tiled=True)
-    student = lax.all_to_all(student_queries, "seq", 1, 0, tiled=True)
-    grad, kl = relation(teacher, student, token_counts)
-    loss = lax.psum(jnp.sum(kl), ("seq", "head")) / (
-        H_REL * jnp.sum(token_counts).astype(jnp.float32)
-    )
-    student_grad = lax.all_to_all(grad, "seq", 0, 1, tiled=True).astype(jnp.float32)
-    return (student_grad, loss)
+    )(me, token_counts, *sources)
+    kl = lax.all_to_all(kl, ("seq", "head"), 0, 0, tiled=True)
+    grads = exchange(grads)
+    grad, loss = pl.pallas_call(
+        functools.partial(unpack_kernel, blocks, live),
+        in_specs=[smem] + [vmem] * (blocks + 1),
+        out_specs=[vmem, vmem],
+        out_shape=[
+            jax.ShapeDtypeStruct((rows, student_queries.shape[1]), f32),
+            jax.ShapeDtypeStruct((1, 128), f32),
+        ],
+        compiler_params=params,
+        name="unpack",
+    )(me, kl, *grads)
+    return (grad, loss[0, 0])
 
 
 def solution(mesh):

time: 113 us -> 73.3 us (0.65)
  blocking collectives: 59 us -> 13 us
  starting transfers between devices: 8.66 us -> 16.1 us
  waiting for transfers between devices: 9.66 us -> 13 us
  between operations: 3.12 us -> 0.69 us
  other arithmetic: 2.33 us -> 0 us
    psum x1 -> x0, blocking collectives: 41.2 us -> none  [local(): lax.psum(jnp.sum(kl), ('seq', 'head'))]
    ppermute x0 -> x14, starting transfers between devices: none -> 16.1 us  [exchange(): lax.ppermute(send, 'seq', [(i, i ^ k) for i in range(blocks)])]
    ppermute x0 -> x14, waiting for transfers between devices: none -> 13 us  [exchange(): lax.ppermute(send, 'seq', [(i, i ^ k) for i in range(blocks)])]
    all_to_all x2 -> x0, waiting for transfers between devices: 9.66 us -> none  [the longest x1 9.66 us: local(): student = lax.all_to_all(student_queries, 'seq', 1, 0, tiled=True)]
    all_to_all x2 -> x0, starting transfers between devices: 8.66 us -> none  [the longest x1 5.17 us: local(): student = lax.all_to_all(student_queries, 'seq', 1, 0, tiled=True)]
    all_to_all x1, blocking collectives: 17.8 us -> 13 us  [local(): kl = lax.all_to_all(kl, ('seq', 'head'), 0, 0, tiled=True)]
    reduce_sum x2 -> x0, other arithmetic: 1.24 us -> none  [the longest x1 0.63 us: local(): jnp.sum(token_counts).astype(jnp.float32)]
    pallas_call x1 -> x3, Pallas kernels: 27.3 us -> 28 us  [the longest x1 26.6 us: local(): pl.pallas_call(functools.partial(relation_kernel, blocks, heads, tiles),...]
  transfers between devices with their start and end apart: 2 -> 14, of which waited for: 1 -> 3; matrix products, arithmetic and copies ran while one was open for 1% -> 0% of each run, Pallas kernels for 0% -> 0%
where the time goes in v2:
time: 73.3 us; the launch traced here: 73 us
  Pallas kernels  28 us (38%)
  starting transfers between devices  16.1 us (22%)
  waiting for transfers between devices  13 us (18%)
  blocking collectives  13 us (18%)
  local copies, waits for them, and re-layouts  2.26 us (3%)
    pallas_call x1, Pallas kernels, local(): pl.pallas_call(functools.partial(relation_kernel, blocks, heads, tiles),...  26.6 us
    ppermute x14, starting transfers between devices, exchange(): lax.ppermute(send, 'seq', [(i, i ^ k) for i in range(blocks)])  16.1 us
    all_to_all x1, blocking collectives, local(): kl = lax.all_to_all(kl, ('seq', 'head'), 0, 0, tiled=True)  13 us
    ppermute x14, waiting for transfers between devices, exchange(): lax.ppermute(send, 'seq', [(i, i ^ k) for i in range(blocks)])  13 us
    unnamed x6, local copies, waits for them, and re-layouts  2.26 us
  transfers between devices with their start and end apart: 14, of which 3 were waited for; matrix products, arithmetic and copies ran while one was open for 0% of the time, Pallas kernels for 0%

profile of v2, /device:TPU:0, one launch (start us, length us, event | category | flops | bytes accessed | tf_op | source)
XLA Modules:
  0.0 73.0 jit_solution(16608234009720238814)
XLA Ops:
  0.6 0.0 copy-start
  0.6 1.2 %copy-done = bf16[256,2048]{1,0:T(8,128)(2,1)S(1)} copy-done((bf16[256,2048]{1,0:T(8,128)(2,1)S(1)}, bf16[256,2048]{1,0:T(8,128)(2,1)}, u32[]{:S(2)}) %copy-start) | copy-done | bytes 1048600
  1.9 0.0 copy-start.1
  1.9 1.0 %copy-done.1 = bf16[256,1024]{1,0:T(8,128)(2,1)S(1)} copy-done((bf16[256,1024]{1,0:T(8,128)(2,1)S(1)}, bf16[256,1024]{1,0:T(8,128)(2,1)}, u32[]{:S(2)}) %copy-start.1) | copy-done | bytes 524312
  2.9 0.3 pack.1
  3.2 0.5 collective-permute-start
  3.7 2.6 %collective-permute-start.1 = (bf16[256,384]{1,0:T(8,128)(2,1)S(1)}, bf16[256,384]{1,0:T(8,128)(2,1)S(1)}, u32[]{:S(2)}, u32[]{:S(2)}) collective-permute-start(bf16[256,384]{1,0:T(8,128)(2,1)S(1)} %get-tuple-element.23), channel_id=1, source_target_pairs={{0,8},{4,12},{8,0},{12,4},{16,24},{20,28},{24,16},{28,20},{1,9},{5... | collective-permute-start | bytes 589832 | tf_op jit(solution)/shard_map/ppermute | solution.py:221
  6.3 0.1 collective-permute-start.2
  6.3 1.8 %collective-permute-start.3 = (bf16[256,384]{1,0:T(8,128)(2,1)S(1)}, bf16[256,384]{1,0:T(8,128)(2,1)S(1)}, u32[]{:S(2)}, u32[]{:S(2)}) collective-permute-start(bf16[256,384]{1,0:T(8,128)(2,1)S(1)} %get-tuple-element.25), channel_id=1, source_target_pairs={{0,16},{4,20},{8,24},{12,28},{16,0},{20,4},{24,8},{28,12},{1,17},{... | collective-permute-start | bytes 589832 | tf_op jit(solution)/shard_map/ppermute | solution.py:221
  8.1 0.0 collective-permute-start.4
  8.1 0.0 collective-permute-done.refs_1_
  8.1 2.6 %collective-permute-start.5 = (bf16[256,384]{1,0:T(8,128)(2,1)S(1)}, bf16[256,384]{1,0:T(8,128)(2,1)S(1)}, u32[]{:S(2)}, u32[]{:S(2)}) collective-permute-start(bf16[256,384]{1,0:T(8,128)(2,1)S(1)} %get-tuple-element.27), channel_id=1, source_target_pairs={{0,24},{4,28},{8,16},{12,20},{16,8},{20,12},{24,0},{28,4},{1,25},{... | collective-permute-start | bytes 589832 | tf_op jit(solution)/shard_map/ppermute | solution.py:221
  10.7 1.3 %collective-permute-done.1.refs_2_ = bf16[256,384]{1,0:T(8,128)(2,1)S(1)} collective-permute-done((bf16[256,384]{1,0:T(8,128)(2,1)S(1)}, bf16[256,384]{1,0:T(8,128)(2,1)S(1)}, u32[]{:S(2)}, u32[]{:S(2)}) %collective-permute-start.1) | collective-permute-done | bytes 196640 | tf_op jit(solution)/shard_map/ppermute | solution.py:221
  12.0 0.0 copy-start.2
  12.0 1.7 %collective-permute-start.6 = (bf16[256,384]{1,0:T(8,128)(2,1)S(1)}, bf16[256,384]{1,0:T(8,128)(2,1)S(1)}, u32[]{:S(2)}, u32[]{:S(2)}) collective-permute-start(bf16[256,384]{1,0:T(8,128)(2,1)S(1)} %get-tuple-element.28), channel_id=1, source_target_pairs={{0,28},{4,24},{8,20},{12,16},{16,12},{20,8},{24,4},{28,0},{1,29},{... | collective-permute-start | bytes 589832 | tf_op jit(solution)/shard_map/ppermute | solution.py:221
  13.7 2.0 %collective-permute-done.2.refs_3_ = bf16[256,384]{1,0:T(8,128)(2,1)S(1)} collective-permute-done((bf16[256,384]{1,0:T(8,128)(2,1)S(1)}, bf16[256,384]{1,0:T(8,128)(2,1)S(1)}, u32[]{:S(2)}, u32[]{:S(2)}) %collective-permute-start.2) | collective-permute-done | bytes 196640 | tf_op jit(solution)/shard_map/ppermute | solution.py:221
  15.7 0.0 collective-permute-done.3.refs_4_
  15.7 9.7 %collective-permute-done.4.refs_5_ = bf16[256,384]{1,0:T(8,128)(2,1)S(1)} collective-permute-done((bf16[256,384]{1,0:T(8,128)(2,1)S(1)}, bf16[256,384]{1,0:T(8,128)(2,1)S(1)}, u32[]{:S(2)}, u32[]{:S(2)}) %collective-permute-start.4) | collective-permute-done | bytes 196640 | tf_op jit(solution)/shard_map/ppermute | solution.py:221
  25.4 0.0 collective-permute-done.5.refs_6_
  25.4 0.0 collective-permute-done.6.refs_7_
  25.4 0.0 copy-done.2
  25.4 26.6 %relation.1 = (bf16[256,128]{1,0:T(8,128)(2,1)S(1)}, bf16[256,128]{1,0:T(8,128)(2,1)S(1)}, bf16[256,128]{1,0:T(8,128)(2,1)S(1)}, bf16[256,128]{1,0:T(8,128)(2,1)...) custom-call(s32[1]{0:T(128)} %bitcast.me_ref, ...), custom_call_target="tpu_custom_call" | custom-call | tf_op jit(solution)/shard_map/relation/pallas_call | solution.py:234
  52.1 0.6 collective-permute-start.7
  52.7 1.7 %collective-permute-start.8 = (bf16[256,128]{1,0:T(8,128)(2,1)S(1)}, bf16[256,128]{1,0:T(8,128)(2,1)S(1)}, u32[]{:S(2)}, u32[]{:S(2)}) collective-permute-start(bf16[256,128]{1,0:T(8,128)(2,1)S(1)} %get-tuple-element.32), channel_id=1, source_target_pairs={{0,8},{4,12},{8,0},{12,4},{16,24},{20,28},{24,16},{28,20},{1,9},{5... | collective-permute-start | bytes 196616 | tf_op jit(solution)/shard_map/ppermute | solution.py:221
  54.4 0.0 collective-permute-start.9
  54.4 1.5 %collective-permute-start.10 = (bf16[256,128]{1,0:T(8,128)(2,1)S(1)}, bf16[256,128]{1,0:T(8,128)(2,1)S(1)}, u32[]{:S(2)}, u32[]{:S(2)}) collective-permute-start(bf16[256,128]{1,0:T(8,128)(2,1)S(1)} %get-tuple-element.34), channel_id=1, source_target_pairs={{0,16},{4,20},{8,24},{12,28},{16,0},{20,4},{24,8},{28,12},{1,17},{... | collective-permute-start | bytes 196616 | tf_op jit(solution)/shard_map/ppermute | solution.py:221
  55.9 0.3 collective-permute-start.11
  56.2 0.0 collective-permute-done.7.refs_1_
  56.2 2.7 %collective-permute-start.12 = (bf16[256,128]{1,0:T(8,128)(2,1)S(1)}, bf16[256,128]{1,0:T(8,128)(2,1)S(1)}, u32[]{:S(2)}, u32[]{:S(2)}) collective-permute-start(bf16[256,128]{1,0:T(8,128)(2,1)S(1)} %get-tuple-element.36), channel_id=1, source_target_pairs={{0,24},{4,28},{8,16},{12,20},{16,8},{20,12},{24,0},{28,4},{1,25},{... | collective-permute-start | bytes 196616 | tf_op jit(solution)/shard_map/ppermute | solution.py:221
  58.9 0.0 collective-permute-done.8.refs_2_
  58.9 0.0 collective-permute-start.13
  58.9 13.0 %all_to_all.11 = f32[32,1,128]{2,1,0:T(1,128)S(1)} all-to-all(f32[32,1,128]{2,1,0:T(1,128)S(1)} %bitcast.8), channel_id=1, replica_groups=mesh['seq'=8,'head'=4] {'seq','head'}, dimensions={0} | all-to-all | bytes 32768 | tf_op jit(solution)/shard_map/all_to_all | solution.py:255
  71.9 0.0 collective-permute-done.9.refs_3_
  71.9 0.0 collective-permute-done.10.refs_4_
  71.9 0.0 collective-permute-done.11.refs_5_
  71.9 0.0 collective-permute-done.12.refs_6_
  71.9 0.0 collective-permute-done.13.refs_7_
  71.9 1.1 %unpack.1 = (f32[256,1024]{1,0:T(8,128)}, f32[1,128]{1,0:T(1,128)}) custom-call(s32[1]{0:T(128)} %bitcast.me_ref, f32[32,128]{1,0:T(8,128)S(1)} %bitcast.7, bf16[256,128]{1,0:T(8,128)(2,1)S(1)} %get-tuple-element.30.refs_0_, bf16[256,128]{1,0:T(8,128)(2,1)S(1)} %collective-permute-done.7.refs_1_, bf16[256,128]{1,0:T(8,128)(2,1)S(1)} %collective-permute-done.8.refs_2_, ...), custom_call_target="tpu_custom_call" | custom-call | tf_op jit(solution)/shard_map/unpack/pallas_call | solution.py:257
Async XLA Ops:
  0.6 1.2 %copy-start = (bf16[256,2048]{1,0:T(8,128)(2,1)S(1)}, bf16[256,2048]{1,0:T(8,128)(2,1)}, u32[]{:S(2)}) copy-start(bf16[256,2048]{1,0:T(8,128)(2,1)} %teacher_ref.1) | copy-start | bytes 3145732
  1.9 1.0 %copy-start.1 = (bf16[256,1024]{1,0:T(8,128)(2,1)S(1)}, bf16[256,1024]{1,0:T(8,128)(2,1)}, u32[]{:S(2)}) copy-start(bf16[256,1024]{1,0:T(8,128)(2,1)} %student_ref.1) | copy-start | bytes 1572868
  3.2 4.9 %collective-permute-start = (bf16[256,384]{1,0:T(8,128)(2,1)S(1)}, bf16[256,384]{1,0:T(8,128)(2,1)S(1)}, u32[]{:S(2)}, u32[]{:S(2)}) collective-permute-start(bf16[256,384]{1,0:T(8,128)(2,1)S(1)} %get-tuple-element.22), channel_id=1, source_target_pairs={{0,4},{4,0},{8,12},{12,8},{16,20},{20,16},{24,28},{28,24},{1,5},{5... | collective-permute-start | bytes 589832 | tf_op jit(solution)/shard_map/ppermute | solution.py:221
  3.7 8.3 %collective-permute-start.1 = (bf16[256,384]{1,0:T(8,128)(2,1)S(1)}, bf16[256,384]{1,0:T(8,128)(2,1)S(1)}, u32[]{:S(2)}, u32[]{:S(2)}) collective-permute-start(bf16[256,384]{1,0:T(8,128)(2,1)S(1)} %get-tuple-element.23), channel_id=1, source_target_pairs={{0,8},{4,12},{8,0},{12,4},{16,24},{20,28},{24,16},{28,20},{1,9},{5... | collective-permute-start | bytes 589832 | tf_op jit(solution)/shard_map/ppermute | solution.py:221
  6.3 9.4 %collective-permute-start.2 = (bf16[256,384]{1,0:T(8,128)(2,1)S(1)}, bf16[256,384]{1,0:T(8,128)(2,1)S(1)}, u32[]{:S(2)}, u32[]{:S(2)}) collective-permute-start(bf16[256,384]{1,0:T(8,128)(2,1)S(1)} %get-tuple-element.24), channel_id=1, source_target_pairs={{0,12},{4,8},{8,4},{12,0},{16,28},{20,24},{24,20},{28,16},{1,13},{... | collective-permute-start | bytes 589832 | tf_op jit(solution)/shard_map/ppermute | solution.py:221
  6.3 9.4 %collective-permute-start.3 = (bf16[256,384]{1,0:T(8,128)(2,1)S(1)}, bf16[256,384]{1,0:T(8,128)(2,1)S(1)}, u32[]{:S(2)}, u32[]{:S(2)}) collective-permute-start(bf16[256,384]{1,0:T(8,128)(2,1)S(1)} %get-tuple-element.25), channel_id=1, source_target_pairs={{0,16},{4,20},{8,24},{12,28},{16,0},{20,4},{24,8},{28,12},{1,17},{... | collective-permute-start | bytes 589832 | tf_op jit(solution)/shard_map/ppermute | solution.py:221
  8.1 17.3 %collective-permute-start.4 = (bf16[256,384]{1,0:T(8,128)(2,1)S(1)}, bf16[256,384]{1,0:T(8,128)(2,1)S(1)}, u32[]{:S(2)}, u32[]{:S(2)}) collective-permute-start(bf16[256,384]{1,0:T(8,128)(2,1)S(1)} %get-tuple-element.26), channel_id=1, source_target_pairs={{0,20},{4,16},{8,28},{12,24},{16,4},{20,0},{24,12},{28,8},{1,21},{... | collective-permute-start | bytes 589832 | tf_op jit(solution)/shard_map/ppermute | solution.py:221
  8.1 17.3 %collective-permute-start.5 = (bf16[256,384]{1,0:T(8,128)(2,1)S(1)}, bf16[256,384]{1,0:T(8,128)(2,1)S(1)}, u32[]{:S(2)}, u32[]{:S(2)}) collective-permute-start(bf16[256,384]{1,0:T(8,128)(2,1)S(1)} %get-tuple-element.27), channel_id=1, source_target_pairs={{0,24},{4,28},{8,16},{12,20},{16,8},{20,12},{24,0},{28,4},{1,25},{... | collective-permute-start | bytes 589832 | tf_op jit(solution)/shard_map/ppermute | solution.py:221
  12.0 13.4 %copy-start.2 = (s32[8]{0:T(128)S(1)}, s32[8]{0:T(128)}, u32[]{:S(2)}) copy-start(s32[8]{0:T(128)} %counts_ref.1) | copy-start | bytes 100
  12.0 13.4 %collective-permute-start.6 = (bf16[256,384]{1,0:T(8,128)(2,1)S(1)}, bf16[256,384]{1,0:T(8,128)(2,1)S(1)}, u32[]{:S(2)}, u32[]{:S(2)}) collective-permute-start(bf16[256,384]{1,0:T(8,128)(2,1)S(1)} %get-tuple-element.28), channel_id=1, source_target_pairs={{0,28},{4,24},{8,20},{12,16},{16,12},{20,8},{24,4},{28,0},{1,29},{... | collective-permute-start | bytes 589832 | tf_op jit(solution)/shard_map/ppermute | solution.py:221
  52.1 4.1 %collective-permute-start.7 = (bf16[256,128]{1,0:T(8,128)(2,1)S(1)}, bf16[256,128]{1,0:T(8,128)(2,1)S(1)}, u32[]{:S(2)}, u32[]{:S(2)}) collective-permute-start(bf16[256,128]{1,0:T(8,128)(2,1)S(1)} %get-tuple-element.31), channel_id=1, source_target_pairs={{0,4},{4,0},{8,12},{12,8},{16,20},{20,16},{24,28},{28,24},{1,5},{5... | collective-permute-start | bytes 196616 | tf_op jit(solution)/shard_map/ppermute | solution.py:221
  52.7 6.2 %collective-permute-start.8 = (bf16[256,128]{1,0:T(8,128)(2,1)S(1)}, bf16[256,128]{1,0:T(8,128)(2,1)S(1)}, u32[]{:S(2)}, u32[]{:S(2)}) collective-permute-start(bf16[256,128]{1,0:T(8,128)(2,1)S(1)} %get-tuple-element.32), channel_id=1, source_target_pairs={{0,8},{4,12},{8,0},{12,4},{16,24},{20,28},{24,16},{28,20},{1,9},{5... | collective-permute-start | bytes 196616 | tf_op jit(solution)/shard_map/ppermute | solution.py:221
  54.4 17.5 %collective-permute-start.9 = (bf16[256,128]{1,0:T(8,128)(2,1)S(1)}, bf16[256,128]{1,0:T(8,128)(2,1)S(1)}, u32[]{:S(2)}, u32[]{:S(2)}) collective-permute-start(bf16[256,128]{1,0:T(8,128)(2,1)S(1)} %get-tuple-element.33), channel_id=1, source_target_pairs={{0,12},{4,8},{8,4},{12,0},{16,28},{20,24},{24,20},{28,16},{1,13},{... | collective-permute-start | bytes 196616 | tf_op jit(solution)/shard_map/ppermute | solution.py:221
  54.4 17.5 %collective-permute-start.10 = (bf16[256,128]{1,0:T(8,128)(2,1)S(1)}, bf16[256,128]{1,0:T(8,128)(2,1)S(1)}, u32[]{:S(2)}, u32[]{:S(2)}) collective-permute-start(bf16[256,128]{1,0:T(8,128)(2,1)S(1)} %get-tuple-element.34), channel_id=1, source_target_pairs={{0,16},{4,20},{8,24},{12,28},{16,0},{20,4},{24,8},{28,12},{1,17},{... | collective-permute-start | bytes 196616 | tf_op jit(solution)/shard_map/ppermute | solution.py:221
  55.9 16.0 %collective-permute-start.11 = (bf16[256,128]{1,0:T(8,128)(2,1)S(1)}, bf16[256,128]{1,0:T(8,128)(2,1)S(1)}, u32[]{:S(2)}, u32[]{:S(2)}) collective-permute-start(bf16[256,128]{1,0:T(8,128)(2,1)S(1)} %get-tuple-element.35), channel_id=1, source_target_pairs={{0,20},{4,16},{8,28},{12,24},{16,4},{20,0},{24,12},{28,8},{1,21},{... | collective-permute-start | bytes 196616 | tf_op jit(solution)/shard_map/ppermute | solution.py:221
  56.2 15.7 %collective-permute-start.12 = (bf16[256,128]{1,0:T(8,128)(2,1)S(1)}, bf16[256,128]{1,0:T(8,128)(2,1)S(1)}, u32[]{:S(2)}, u32[]{:S(2)}) collective-permute-start(bf16[256,128]{1,0:T(8,128)(2,1)S(1)} %get-tuple-element.36), channel_id=1, source_target_pairs={{0,24},{4,28},{8,16},{12,20},{16,8},{20,12},{24,0},{28,4},{1,25},{... | collective-permute-start | bytes 196616 | tf_op jit(solution)/shard_map/ppermute | solution.py:221
  58.9 13.0 %collective-permute-start.13 = (bf16[256,128]{1,0:T(8,128)(2,1)S(1)}, bf16[256,128]{1,0:T(8,128)(2,1)S(1)}, u32[]{:S(2)}, u32[]{:S(2)}) collective-permute-start(bf16[256,128]{1,0:T(8,128)(2,1)S(1)} %get-tuple-element.37), channel_id=1, source_target_pairs={{0,28},{4,24},{8,20},{12,16},{16,12},{20,8},{24,4},{28,0},{1,29},{... | collective-permute-start | bytes 196616 | tf_op jit(solution)/shard_map/ppermute | solution.py:221

commit v3 on v2

v3 whole, which is shorter than its diff:
```python
import functools
import math

import jax
import jax.numpy as jnp
from jax import lax
from jax.experimental import pallas as pl
from jax.experimental.pallas import tpu as pltpu
from jax.sharding import PartitionSpec as P

DT = 8192
DS = 4096
H_REL = 128
TEACHER_DIM = DT // H_REL
STUDENT_DIM = DS // H_REL

NEGATIVE = -1e30
LOG2E = math.log2(math.e)
TEACHER_SCALE = LOG2E * TEACHER_DIM**-0.5
STUDENT_SCALE = LOG2E * STUDENT_DIM**-0.5
PAD = 8
LANES = 128
TAIL = 16
DEPTH = 256
SAFE_NORM = 320.0


def split_high_low(values):
    high = values.astype(jnp.bfloat16)
    low = (values - high.astype(jnp.float32)).astype(jnp.bfloat16)
    return high, low


def split_three(values):
    high = values.astype(jnp.bfloat16)
    rest = values - high.astype(jnp.float32)
    return (high,) + split_high_low(rest)


def at_columns(index, count, width, act):
    if width % LANES == 0:
        act(pl.ds(pl.multiple_of(index * width, LANES), width))
    else:
        for part in range(count):
            pl.when(index == part)(functools.partial(act, pl.ds(part * width, width)))


def pack_kernel(blocks, me_ref, teacher_ref, student_ref, *sends):
    teacher_width = teacher_ref.shape[1] // blocks
    student_width = student_ref.shape[1] // blocks
    for k in range(blocks):
        to = jnp.bitwise_xor(me_ref[0], k)

        def put_teacher(columns, send=sends[k]):
            send[:, :teacher_width] = teacher_ref[:, columns]

        def put_student(columns, send=sends[k]):
            send[:, teacher_width:] = student_ref[:, columns]

        at_columns(to, blocks, teacher_width, put_teacher)
        at_columns(to, blocks, student_width, put_student)


def pair_sum(parts):
    while len(parts) > 1:
        parts = [a + b for a, b in zip(parts[::2], parts[1::2])]
    return parts[0]


def sum_kernel(*refs):
    total = pair_sum([ref[...].astype(jnp.float32) for ref in refs[:-1]])
    refs[-1][...] = jnp.sum(total, axis=0, keepdims=True)


def unpack_kernel(blocks, me_ref, *refs):
    grad_ref = refs[blocks]
    for k in range(blocks):

        def put(columns, source=refs[k]):
            grad_ref[:, columns] = source[: grad_ref.shape[0], :].astype(jnp.float32)

        at_columns(jnp.bitwise_xor(me_ref[0], k), blocks, refs[k].shape[1], put)


def fold(values):
    rows, columns = values.shape
    return jnp.sum(values.reshape(rows // 8, 8, columns), axis=0)


def relation_kernel(blocks, heads, tiles, me_ref, counts_ref, *refs):
    sources = refs[:blocks]
    grads = refs[blocks : 2 * blocks]
    (
        pack,
        key_op,
        row_op,
        student_col,
        teacher_prob,
        student_prob,
        grad_cols,
        grad_rows,
        kl_sum,
    ) = refs[2 * blocks :]
    f32, bf16 = jnp.float32, jnp.bfloat16
    rows = sources[0].shape[0]
    live = tiles * rows
    window = rows + PAD
    student_at = heads * TEACHER_DIM
    filled = 2 * TEACHER_DIM + 2 * STUDENT_DIM

    position = lax.broadcasted_iota(jnp.int32, (window, rows), 0)
    token = lax.broadcasted_iota(jnp.int32, (window, rows), 1)
    pack[...] = jnp.zeros(pack.shape, f32)
    places = []
    for k in range(blocks):
        owner = jnp.bitwise_xor(me_ref[0], k)
        start = sum(jnp.where(b < owner, counts_ref[b], 0) for b in range(blocks))
        base = pl.multiple_of(start // PAD * PAD, PAD)
        places.append((base, start - base, counts_ref[owner]))
    for source, (base, shift, count) in zip(sources, places):
        place = ((position == token + shift) & (token < count)).astype(bf16)
        moved = jnp.dot(place, source[...], preferred_element_type=f32)
        pack[pl.ds(base, window), :] = pack[pl.ds(base, window), :] + moved

    ones = jnp.ones((rows, DEPTH - filled), bf16)
    spare = lax.broadcasted_iota(jnp.int32, (DEPTH - filled, rows), 0)
    teacher_gap = jnp.zeros((2 * STUDENT_DIM, rows), bf16)
    student_gap = jnp.zeros((2 * TEACHER_DIM, rows), bf16)
    norms = []

    def shift_rows(norm):
        parts = [part.astype(f32) for part in split_three(-norm)]
        out = jnp.where(spare == 0, parts[0], 0.0)
        out = jnp.where(spare == 1, parts[1], out)
        return jnp.where(spare == 2, parts[2], out).astype(bf16)

    for i in range(tiles):
        here = pl.ds(i * rows, rows)
        tile = pack[here, :]
        tile_t = tile.T
        tile_b = tile.astype(bf16)
        for h in range(heads):
            tb = tile_b[:, h * TEACHER_DIM : (h + 1) * TEACHER_DIM]
            at = student_at + h * STUDENT_DIM
            sb = tile_b[:, at : at + STUDENT_DIM]
            key_op[h, here, :] = jnp.concatenate([tb, tb, sb, sb, ones], axis=1)
            teacher_t = tile_t[h * TEACHER_DIM : (h + 1) * TEACHER_DIM, :]
            student_t = tile_t[at : at + STUDENT_DIM, :]
            student_col[h, i] = student_t.astype(bf16)
            teacher_norm = TEACHER_SCALE * jnp.sum(teacher_t * teacher_t, axis=0, keepdims=True)
            student_norm = STUDENT_SCALE * jnp.sum(student_t * student_t, axis=0, keepdims=True)
            norms += [teacher_norm, student_norm]
            high, low = split_high_low(teacher_t * TEACHER_SCALE)
            teacher_op = [high, low, teacher_gap, shift_rows(teacher_norm)]
            row_op[h, i, :, :rows] = jnp.concatenate(teacher_op, axis=0)
            high, low = split_high_low(student_t * STUDENT_SCALE)
            student_op = [student_gap, high, low, shift_rows(student_norm)]
            row_op[h, i, :, rows:] = jnp.concatenate(student_op, axis=0)

    safe = jnp.max(functools.reduce(jnp.maximum, norms)) <= SAFE_NORM
    key_pos = lax.broadcasted_iota(jnp.int32, (rows, rows), 0)
    row_pos = lax.broadcasted_iota(jnp.int32, (rows, rows), 1)

    def logits(h, i, j):
        keys = pl.ds(pl.multiple_of(j * rows, rows), rows)
        both = jnp.dot(key_op[h, keys, :], row_op[h, i], preferred_element_type=f32)
        return both[:, :rows], both[:, rows:]

    def row_term(h, j, weights):
        return jnp.dot(student_col[h, j], weights, preferred_element_type=f32)

    def key_term(h, i, weights):
        return lax.dot_general(
            student_col[h, i], weights, (((1,), (1,)), ((), ())), preferred_element_type=f32
        )

    @pl.when(safe)
    def shifted_by_own_logit():
        def head_step(h, kl_total):
            for i in range(tiles):
                teacher_sum = student_sum = cross_sum = jnp.zeros((8, rows), f32)
                for j in range(i + 1):
                    teacher, student = logits(h, i, j)
                    if i == j:
                        teacher = jnp.where(key_pos <= row_pos, teacher, NEGATIVE)
                        student = jnp.where(key_pos <= row_pos, student, NEGATIVE)
                    teacher_exp = jnp.exp2(teacher)
                    student_exp = jnp.exp2(student)
                    teacher_prob[j] = teacher_exp
                    student_prob[j] = student_exp
                    teacher_sum = teacher_sum + fold(teacher_exp)
                    student_sum = student_sum + fold(student_exp)
                    cross_sum = cross_sum + fold(teacher_exp * (teacher - student))
                teacher_sum = jnp.sum(teacher_sum, axis=0, keepdims=True)
                student_sum = jnp.sum(student_sum, axis=0, keepdims=True)
                cross_sum = jnp.sum(cross_sum, axis=0, keepdims=True)
                teacher_inv = 1.0 / teacher_sum
                student_inv = 1.0 / student_sum
                kl_total = kl_total + (
                    cross_sum * teacher_inv - jnp.log2(teacher_sum) + jnp.log2(student_sum)
                )
                row_grad = jnp.zeros((STUDENT_DIM, rows), f32)
                for j in range(i + 1):
                    weights = (
                        student_prob[j] * student_inv - teacher_prob[j] * teacher_inv
                    ).astype(bf16)
                    row_grad = row_grad + row_term(h, j, weights)
                    key_grad = key_term(h, i, weights)
                    if j < i:
                        grad_cols[h, j] = grad_cols[h, j] + key_grad
                    else:
                        grad_cols[h, i] = row_grad + key_grad
            return kl_total

        kl_sum[...] = lax.fori_loop(0, heads, head_step, jnp.zeros((1, rows), f32))

    @pl.when(jnp.logical_not(safe))
    def shifted_by_maximum():
        kl_sum[...] = jnp.zeros((1, rows), f32)
        grad_cols[...] = jnp.zeros(grad_cols.shape, f32)

        def masked(h, i, j):
            allowed = key_pos + j * rows <= row_pos + i * rows
            teacher, student = logits(h, i, j)
            return jnp.where(allowed, teacher, NEGATIVE), jnp.where(allowed, student, NEGATIVE)

        def row_step(step, _):
            h, i = step // tiles, step % tiles

            def advance(j, state):
                teacher_max, teacher_sum, cross_sum, student_max, student_sum = state
                teacher, student = masked(h, i, j)
                teacher_top = jnp.maximum(teacher_max, jnp.max(teacher, axis=0, keepdims=True))
                student_top = jnp.maximum(student_max, jnp.max(student, axis=0, keepdims=True))
                teacher_exp = jnp.exp2(teacher - teacher_top)
                student_exp = jnp.exp2(student - student_top)
                shrink = jnp.exp2(teacher_max - teacher_top)
                cross = jnp.sum(teacher_exp * (teacher - student), axis=0, keepdims=True)
                return (
                    teacher_top,
                    teacher_sum * shrink + jnp.sum(teacher_exp, axis=0, keepdims=True),
                    cross_sum * shrink + cross,
                    student_top,
                    student_sum * jnp.exp2(student_max - student_top)
                    + jnp.sum(student_exp, axis=0, keepdims=True),
                )

            lowest = jnp.full((1, rows), NEGATIVE, f32)
            zeros = jnp.zeros((1, rows), f32)
            teacher_max, teacher_sum, cross_sum, student_max, student_sum = lax.fori_loop(
                0, i + 1, advance, (lowest, zeros, zeros, lowest, zeros)
            )
            teacher_lse = teacher_max + jnp.log2(teacher_sum)
            student_lse = student_max + jnp.log2(student_sum)
            kl_sum[...] = kl_sum[...] + (cross_sum / teacher_sum - teacher_lse + student_lse)

            def spread(j, row_grad):
                teacher, student = masked(h, i, j)
                weights = jnp.exp2(student - student_lse) - jnp.exp2(teacher - teacher_lse)
                weights = weights.astype(bf16)
                grad_cols[h, j] = grad_cols[h, j] + key_term(h, i, weights)
                return row_grad + row_term(h, j, weights)

            row_grad = lax.fori_loop(0, i + 1, spread, jnp.zeros((STUDENT_DIM, rows), f32))
            grad_cols[h, i] = grad_cols[h, i] + row_grad
            return 0

        lax.fori_loop(0, heads * tiles, row_step, 0)

    for i in range(tiles):
        columns = grad_cols[:, i].reshape(heads * STUDENT_DIM, rows)
        grad_rows[pl.ds(i * rows, rows), :] = columns.T * (STUDENT_DIM**-0.5)
    grad_rows[pl.ds(live, window), :] = jnp.zeros((window, heads * STUDENT_DIM), f32)
    divergence = jnp.sum(kl_sum[...], axis=1, keepdims=True) * math.log(2.0)
    parts = [part.astype(f32) for part in split_three(divergence)]
    line = lax.broadcasted_iota(jnp.int32, (TAIL, heads * STUDENT_DIM), 0)
    tail = jnp.where(line == 0, parts[0], 0.0)
    tail = jnp.where(line == 1, parts[1], tail)
    tail = jnp.where(line == 2, parts[2], tail).astype(bf16)
    position = lax.broadcasted_iota(jnp.int32, (rows, window), 1)
    token = lax.broadcasted_iota(jnp.int32, (rows, window), 0)
    for grad, (base, shift, count) in zip(grads, places):
        place = ((position == token + shift) & (token < count)).astype(bf16)
        block = grad_rows[pl.ds(base, window), :].astype(bf16)
        grad[:rows, :] = jnp.dot(place, block, preferred_element_type=f32).astype(bf16)
        grad[rows:, :] = tail


def local(teacher_queries, student_queries, token_counts):
    f32, bf16 = jnp.float32, jnp.bfloat16
    blocks = lax.axis_size("seq")
    rows = teacher_queries.shape[0]
    heads = teacher_queries.shape[1] // TEACHER_DIM // blocks
    tiles = blocks * 3 // 4
    live = tiles * rows
    width = heads * (TEACHER_DIM + STUDENT_DIM)
    vmem = pl.BlockSpec(memory_space=pltpu.VMEM)
    smem = pl.BlockSpec(memory_space=pltpu.SMEM)
    params = pltpu.CompilerParams(vmem_limit_bytes=48 * 1024 * 1024)
    me = lax.axis_index("seq").reshape(1)

    far_first = sorted(range(1, blocks), key=lambda k: -(k >> 1).bit_count())

    def exchange(sends):
        out = list(sends)
        for k in far_first:
            out[k] = lax.ppermute(sends[k], "seq", [(i, i ^ k) for i in range(blocks)])
        return out

    sends = pl.pallas_call(
        functools.partial(pack_kernel, blocks),
        in_specs=[smem, vmem, vmem],
        out_specs=[vmem] * blocks,
        out_shape=[jax.ShapeDtypeStruct((rows, width), bf16)] * blocks,
        compiler_params=params,
        name="pack",
    )(me, teacher_queries, student_queries)
    sources = exchange(sends)
    grads = pl.pallas_call(
        functools.partial(relation_kernel, blocks, heads, tiles),
        in_specs=[smem, smem] + [vmem] * blocks,
        out_specs=[vmem] * blocks,
        out_shape=[jax.ShapeDtypeStruct((rows + TAIL, heads * STUDENT_DIM), bf16)] * blocks,
        scratch_shapes=[
            pltpu.VMEM((live + rows + PAD, width), f32),
            pltpu.VMEM((heads, live, DEPTH), bf16),
            pltpu.VMEM((heads, tiles, DEPTH, 2 * rows), bf16),
            pltpu.VMEM((heads, tiles, STUDENT_DIM, rows), bf16),
            pltpu.VMEM((tiles, rows, rows), f32),
            pltpu.VMEM((tiles, rows, rows), f32),
            pltpu.VMEM((heads, tiles, STUDENT_DIM, rows), f32),
            pltpu.VMEM((live + rows + PAD, heads * STUDENT_DIM), f32),
            pltpu.VMEM((1, rows), f32),
        ],
        compiler_params=params,
        name="relation",
    )(me, token_counts, *sources)
    grads = exchange(grads)
    kl = pl.pallas_call(
        sum_kernel,
        grid=(1,),
        in_specs=[pl.BlockSpec((TAIL, heads * STUDENT_DIM), lambda _: (rows // TAIL, 0))] * blocks,
        out_specs=pl.BlockSpec((1, heads * STUDENT_DIM), lambda _: (0, 0)),
        out_shape=jax.ShapeDtypeStruct((1, heads * STUDENT_DIM), f32),
        name="sum_kl",
    )(*grads)
    groups = lax.axis_size("head")
    total = pair_sum(
        [kl]
        + [
            lax.ppermute(kl, "head", [(i, i ^ k) for i in range(groups)])
            for k in range(1, groups)
        ]
    )
    grad = pl.pallas_call(
        functools.partial(unpack_kernel, blocks),
        in_specs=[smem] + [vmem] * blocks,
        out_specs=vmem,
        out_shape=jax.ShapeDtypeStruct((rows, student_queries.shape[1]), f32),
        compiler_params=params,
        name="unpack",
    )(me, *grads)
    return (grad, total[0, 0] / (H_REL * jnp.sum(token_counts).astype(f32)))


def solution(mesh):
    return jax.shard_map(
        local,
        mesh=mesh,
        in_specs=(P("seq", "head"), P("seq", "head"), P()),
        out_specs=(P("seq", "head"), P()),
        check_vma=False,
    )
```

time: 73.3 us -> 120 us (1.64)
  starting transfers between devices: 16.1 us -> 64.3 us
  blocking collectives: 13 us -> 0 us
  local copies, waits for them, and re-layouts: 2.26 us -> 9.66 us
  waiting for transfers between devices: 13 us -> 17.5 us
  Pallas kernels: 28 us -> 24 us
  between operations: 0.69 us -> 2.56 us
    ppermute x14 -> x17, starting transfers between devices: 16.1 us -> 64.3 us  [the longest x14 59.9 us: exchange(): out[k] = lax.ppermute(sends[k], 'seq', [(i, i ^ k) for i in range(blocks)])]
    all_to_all x1 -> x0, blocking collectives: 13 us -> none  [local(): kl = lax.all_to_all(kl, ('seq', 'head'), 0, 0, tiled=True)]
    unnamed x6 -> x40, local copies, waits for them, and re-layouts: 2.26 us -> 9.66 us
    pallas_call x1, Pallas kernels: 26.6 us -> 21.3 us  [local(): pl.pallas_call(functools.partial(relation_kernel, blocks, heads, tiles),...]
    ppermute x14 -> x17, waiting for transfers between devices: 13 us -> 17.5 us  [the longest x14 17.5 us: exchange(): out[k] = lax.ppermute(sends[k], 'seq', [(i, i ^ k) for i in range(blocks)])]
    pallas_call x1 -> x2, Pallas kernels: 1.1 us -> 2.44 us  [the longest x1 1.35 us: local(): pl.pallas_call(sum_kernel, grid=(1,), in_specs=[pl.BlockSpec((TAIL, heads...]
  transfers between devices with their start and end apart: 14 -> 17, of which waited for: 3 -> 6; matrix products, arithmetic and copies ran while one was open for 0% -> 1% of each run, Pallas kernels for 0% -> 1%
where the time goes in v3:
time: 120 us; the launch traced here: 119 us
  starting transfers between devices  64.3 us (54%)
  Pallas kernels  24 us (20%)
  waiting for transfers between devices  17.5 us (15%)
  local copies, waits for them, and re-layouts  9.66 us (8%)
  between operations  2.56 us (2%)
    ppermute x14, starting transfers between devices, exchange(): out[k] = lax.ppermute(sends[k], 'seq', [(i, i ^ k) for i in range(blocks)])  59.9 us
    pallas_call x1, Pallas kernels, local(): pl.pallas_call(functools.partial(relation_kernel, blocks, heads, tiles),...  21.3 us
    ppermute x14, waiting for transfers between devices, exchange(): out[k] = lax.ppermute(sends[k], 'seq', [(i, i ^ k) for i in range(blocks)])  17.5 us
    unnamed x40, local copies, waits for them, and re-layouts  9.66 us
    ppermute x3, starting transfers between devices, local(): lax.ppermute(kl, 'head', [(i, i ^ k) for i in range(groups)])  4.38 us
  transfers between devices with their start and end apart: 17, of which 6 were waited for; matrix products, arithmetic and copies ran while one was open for 1% of the time, Pallas kernels for 1%

profile of v3, /device:TPU:0, one launch (start us, length us, event | category | flops | bytes accessed | tf_op | source)
XLA Modules:
  0.0 118.6 jit_solution(3256245217929652622)
XLA Ops:
  0.6 1.2 %copy-done = bf16[256,2048]{1,0:T(8,128)(2,1)S(1)} copy-done((bf16[256,2048]{1,0:T(8,128)(2,1)S(1)}, bf16[256,2048]{1,0:T(8,128)(2,1)}, u32[]{:S(2)}) %copy-start) | copy-done | bytes 1048600
  1.9 1.0 copy-done.1
  2.9 0.3 pack.1
  3.2 0.5 collective-permute-start
  3.7 2.6 %collective-permute-start.1 = (bf16[256,384]{1,0:T(8,128)(2,1)S(1)}, bf16[256,384]{1,0:T(8,128)(2,1)S(1)}, u32[]{:S(2)}, u32[]{:S(2)}) collective-permute-start(bf16[256,384]{1,0:T(8,128)(2,1)S(1)} %get-tuple-element.20), channel_id=1, source_target_pairs={{0,8},{4,12},{8,0},{12,4},{16,24},{20,28},{24,16},{28,20},{1,9},{5... | collective-permute-start | bytes 589832 | tf_op jit(solution)/shard_map/ppermute | solution.py:307
  6.3 0.1 collective-permute-start.2
  6.3 1.8 %collective-permute-start.3 = (bf16[256,384]{1,0:T(8,128)(2,1)S(1)}, bf16[256,384]{1,0:T(8,128)(2,1)S(1)}, u32[]{:S(2)}, u32[]{:S(2)}) collective-permute-start(bf16[256,384]{1,0:T(8,128)(2,1)S(1)} %get-tuple-element.22), channel_id=1, source_target_pairs={{0,16},{4,20},{8,24},{12,28},{16,0},{20,4},{24,8},{28,12},{1,17},{... | collective-permute-start | bytes 589832 | tf_op jit(solution)/shard_map/ppermute | solution.py:307
  8.1 0.0 collective-permute-start.4
  8.1 0.0 collective-permute-done.refs_1_
  8.1 2.6 %collective-permute-start.5 = (bf16[256,384]{1,0:T(8,128)(2,1)S(1)}, bf16[256,384]{1,0:T(8,128)(2,1)S(1)}, u32[]{:S(2)}, u32[]{:S(2)}) collective-permute-start(bf16[256,384]{1,0:T(8,128)(2,1)S(1)} %get-tuple-element.24), channel_id=1, source_target_pairs={{0,24},{4,28},{8,16},{12,20},{16,8},{20,12},{24,0},{28,4},{1,25},{... | collective-permute-start | bytes 589832 | tf_op jit(solution)/shard_map/ppermute | solution.py:307
  10.7 1.3 %collective-permute-done.1.refs_2_ = bf16[256,384]{1,0:T(8,128)(2,1)S(1)} collective-permute-done((bf16[256,384]{1,0:T(8,128)(2,1)S(1)}, bf16[256,384]{1,0:T(8,128)(2,1)S(1)}, u32[]{:S(2)}, u32[]{:S(2)}) %collective-permute-start.1) | collective-permute-done | bytes 196640 | tf_op jit(solution)/shard_map/ppermute | solution.py:307
  12.0 1.7 %collective-permute-start.6 = (bf16[256,384]{1,0:T(8,128)(2,1)S(1)}, bf16[256,384]{1,0:T(8,128)(2,1)S(1)}, u32[]{:S(2)}, u32[]{:S(2)}) collective-permute-start(bf16[256,384]{1,0:T(8,128)(2,1)S(1)} %get-tuple-element.25), channel_id=1, source_target_pairs={{0,28},{4,24},{8,20},{12,16},{16,12},{20,8},{24,4},{28,0},{1,29},{... | collective-permute-start | bytes 589832 | tf_op jit(solution)/shard_map/ppermute | solution.py:307
  13.7 2.0 %collective-permute-done.2.refs_3_ = bf16[256,384]{1,0:T(8,128)(2,1)S(1)} collective-permute-done((bf16[256,384]{1,0:T(8,128)(2,1)S(1)}, bf16[256,384]{1,0:T(8,128)(2,1)S(1)}, u32[]{:S(2)}, u32[]{:S(2)}) %collective-permute-start.2) | collective-permute-done | bytes 196640 | tf_op jit(solution)/shard_map/ppermute | solution.py:307
  15.7 0.0 collective-permute-done.3.refs_4_
  15.7 9.7 %collective-permute-done.4.refs_5_ = bf16[256,384]{1,0:T(8,128)(2,1)S(1)} collective-permute-done((bf16[256,384]{1,0:T(8,128)(2,1)S(1)}, bf16[256,384]{1,0:T(8,128)(2,1)S(1)}, u32[]{:S(2)}, u32[]{:S(2)}) %collective-permute-start.4) | collective-permute-done | bytes 196640 | tf_op jit(solution)/shard_map/ppermute | solution.py:307
  25.4 0.0 collective-permute-done.5.refs_6_
  25.4 0.0 collective-permute-done.6.refs_7_
  25.4 21.3 %relation.1 = (bf16[272,128]{1,0:T(8,128)(2,1)S(1)}, bf16[272,128]{1,0:T(8,128)(2,1)S(1)}, bf16[272,128]{1,0:T(8,128)(2,1)S(1)}, bf16[272,128]{1,0:T(8,128)(2,1)...) custom-call(s32[1]{0:T(128)} %bitcast.me_ref, ...), custom_call_target="tpu_custom_call" | custom-call | tf_op jit(solution)/shard_map/relation/pallas_call | solution.py:319
  46.7 0.0 copy-start.2
  46.7 0.6 copy-done.2
  47.3 1.9 %collective-permute-start.10 = (bf16[272,128]{1,0:T(8,128)(2,1)S(1)}, bf16[272,128]{1,0:T(8,128)(2,1)S(1)}, u32[]{:S(2)}, u32[]{:S(2)}) collective-permute-start(bf16[272,128]{1,0:T(8,128)(2,1)S(1)} %get-tuple-element.30), channel_id=1, source_target_pairs={{0,16},{4,20},{8,24},{12,28},{16,0},{20,4},{24,8},{28,12},{1,17},{... | collective-permute-start | bytes 208904 | tf_op jit(solution)/shard_map/ppermute | solution.py:307
  49.2 0.1 collective-permute-start.11
  49.3 45.1 %collective-permute-start.12 = (bf16[272,128]{1,0:T(8,128)(2,1)S(1)}, bf16[272,128]{1,0:T(8,128)(2,1)S(1)}, u32[]{:S(2)}, u32[]{:S(2)}) collective-permute-start(bf16[272,128]{1,0:T(8,128)(2,1)S(1)} %get-tuple-element.32), channel_id=1, source_target_pairs={{0,24},{4,28},{8,16},{12,20},{16,8},{20,12},{24,0},{28,4},{1,25},{... | collective-permute-start | bytes 208904 | tf_op jit(solution)/shard_map/ppermute | solution.py:307
  94.3 1.8 %collective-permute-start.13 = (bf16[272,128]{1,0:T(8,128)(2,1)S(1)}, bf16[272,128]{1,0:T(8,128)(2,1)S(1)}, u32[]{:S(2)}, u32[]{:S(2)}) collective-permute-start(bf16[272,128]{1,0:T(8,128)(2,1)S(1)} %get-tuple-element.33), channel_id=1, source_target_pairs={{0,28},{4,24},{8,20},{12,16},{16,12},{20,8},{24,4},{28,0},{1,29},{... | collective-permute-start | bytes 208904 | tf_op jit(solution)/shard_map/ppermute | solution.py:307
  96.1 0.1 collective-permute-start.7
  96.2 1.7 %collective-permute-start.8 = (bf16[272,128]{1,0:T(8,128)(2,1)S(1)}, bf16[272,128]{1,0:T(8,128)(2,1)S(1)}, u32[]{:S(2)}, u32[]{:S(2)}) collective-permute-start(bf16[272,128]{1,0:T(8,128)(2,1)S(1)} %get-tuple-element.28), channel_id=1, source_target_pairs={{0,8},{4,12},{8,0},{12,4},{16,24},{20,28},{24,16},{28,20},{1,9},{5... | collective-permute-start | bytes 208904 | tf_op jit(solution)/shard_map/ppermute | solution.py:307
  97.9 0.0 collective-permute-done.11.refs_5_
  98.0 0.0 collective-permute-start.9
  98.0 0.0 collective-permute-done.12.refs_6_
  98.0 1.0 collective-permute-done.13.refs_7_
  99.0 0.0 collective-permute-done.7.refs_1_
  99.0 2.8 %collective-permute-done.8.refs_2_ = bf16[272,128]{1,0:T(8,128)(2,1)S(1)} collective-permute-done((bf16[272,128]{1,0:T(8,128)(2,1)S(1)}, bf16[272,128]{1,0:T(8,128)(2,1)S(1)}, u32[]{:S(2)}, u32[]{:S(2)}) %collective-permute-start.8) | collective-permute-done | bytes 69664 | tf_op jit(solution)/shard_map/ppermute | solution.py:307
  101.8 0.7 collective-permute-done.9.refs_3_
  102.6 0.6 copy-done.16
  103.1 1.4 %sum_kl.1 = f32[1,128]{1,0:T(1,128)} custom-call(bf16[272,128]{1,0:T(8,128)(2,1)} %copy-done.2, bf16[272,128]{1,0:T(8,128)(2,1)} %copy-done.12, bf16[272,128]{1,0:T(8,128)(2,1)} %copy-done.14, bf16[272,128]{1,0:T(8,128)(2,1)} %copy-done.16, bf16[272,128]{1,0:T(8,128)(2,1)} %copy-done.4, bf16[272,128]{1,0:T(8,128)(2,1)} %copy-done.6, ...), custom_call_target="tpu_custom_call" | custom-call | tf_op jit(solution)/shard_map/sum_kl/pallas_call | solution.py:339
  104.5 4.4 %collective-permute-start.16 = (f32[1,128]{1,0:T(1,128)}, f32[1,128]{1,0:T(1,128)S(1)}, u32[]{:S(2)}, u32[]{:S(2)}) collective-permute-start(f32[1,128]{1,0:T(1,128)} %sum_kl.1), channel_id=1, source_target_pairs={{0,3},{1,2},{2,1},{3,0},{4,7},{5,6},{6,5},{7,4},{8,11},{9,10},{10,... | collective-permute-start | bytes 1544 | tf_op jit(solution)/shard_map/ppermute | solution.py:351
  108.9 0.6 reduce_sum.9
  110.2 0.9 copy-done.5
  111.0 0.9 copy-done.7
  111.9 0.9 copy-done.9
  112.8 0.9 copy-done.11
  113.7 0.9 copy-done.13
  114.6 0.9 copy-done.15
  115.5 0.9 copy-done.17
  116.3 1.1 unpack.1
  117.4 0.0 collective-permute-done.14
  117.4 0.0 collective-permute-done.15
  117.4 0.0 collective-permute-done.16
  (32 shorter events, 0.1 us)
Async XLA Ops:
  0.6 1.2 %copy-start = (bf16[256,2048]{1,0:T(8,128)(2,1)S(1)}, bf16[256,2048]{1,0:T(8,128)(2,1)}, u32[]{:S(2)}) copy-start(bf16[256,2048]{1,0:T(8,128)(2,1)} %teacher_ref.1) | copy-start | bytes 3145732
  1.9 1.0 copy-start.1
  3.2 4.9 %collective-permute-start = (bf16[256,384]{1,0:T(8,128)(2,1)S(1)}, bf16[256,384]{1,0:T(8,128)(2,1)S(1)}, u32[]{:S(2)}, u32[]{:S(2)}) collective-permute-start(bf16[256,384]{1,0:T(8,128)(2,1)S(1)} %get-tuple-element.19), channel_id=1, source_target_pairs={{0,4},{4,0},{8,12},{12,8},{16,20},{20,16},{24,28},{28,24},{1,5},{5... | collective-permute-start | bytes 589832 | tf_op jit(solution)/shard_map/ppermute | solution.py:307
  3.7 8.3 %collective-permute-start.1 = (bf16[256,384]{1,0:T(8,128)(2,1)S(1)}, bf16[256,384]{1,0:T(8,128)(2,1)S(1)}, u32[]{:S(2)}, u32[]{:S(2)}) collective-permute-start(bf16[256,384]{1,0:T(8,128)(2,1)S(1)} %get-tuple-element.20), channel_id=1, source_target_pairs={{0,8},{4,12},{8,0},{12,4},{16,24},{20,28},{24,16},{28,20},{1,9},{5... | collective-permute-start | bytes 589832 | tf_op jit(solution)/shard_map/ppermute | solution.py:307
  6.3 9.4 %collective-permute-start.2 = (bf16[256,384]{1,0:T(8,128)(2,1)S(1)}, bf16[256,384]{1,0:T(8,128)(2,1)S(1)}, u32[]{:S(2)}, u32[]{:S(2)}) collective-permute-start(bf16[256,384]{1,0:T(8,128)(2,1)S(1)} %get-tuple-element.21), channel_id=1, source_target_pairs={{0,12},{4,8},{8,4},{12,0},{16,28},{20,24},{24,20},{28,16},{1,13},{... | collective-permute-start | bytes 589832 | tf_op jit(solution)/shard_map/ppermute | solution.py:307
  6.3 9.4 %collective-permute-start.3 = (bf16[256,384]{1,0:T(8,128)(2,1)S(1)}, bf16[256,384]{1,0:T(8,128)(2,1)S(1)}, u32[]{:S(2)}, u32[]{:S(2)}) collective-permute-start(bf16[256,384]{1,0:T(8,128)(2,1)S(1)} %get-tuple-element.22), channel_id=1, source_target_pairs={{0,16},{4,20},{8,24},{12,28},{16,0},{20,4},{24,8},{28,12},{1,17},{... | collective-permute-start | bytes 589832 | tf_op jit(solution)/shard_map/ppermute | solution.py:307
  8.1 17.3 %collective-permute-start.4 = (bf16[256,384]{1,0:T(8,128)(2,1)S(1)}, bf16[256,384]{1,0:T(8,128)(2,1)S(1)}, u32[]{:S(2)}, u32[]{:S(2)}) collective-permute-start(bf16[256,384]{1,0:T(8,128)(2,1)S(1)} %get-tuple-element.23), channel_id=1, source_target_pairs={{0,20},{4,16},{8,28},{12,24},{16,4},{20,0},{24,12},{28,8},{1,21},{... | collective-permute-start | bytes 589832 | tf_op jit(solution)/shard_map/ppermute | solution.py:307
  8.1 17.3 %collective-permute-start.5 = (bf16[256,384]{1,0:T(8,128)(2,1)S(1)}, bf16[256,384]{1,0:T(8,128)(2,1)S(1)}, u32[]{:S(2)}, u32[]{:S(2)}) collective-permute-start(bf16[256,384]{1,0:T(8,128)(2,1)S(1)} %get-tuple-element.24), channel_id=1, source_target_pairs={{0,24},{4,28},{8,16},{12,20},{16,8},{20,12},{24,0},{28,4},{1,25},{... | collective-permute-start | bytes 589832 | tf_op jit(solution)/shard_map/ppermute | solution.py:307
  12.0 13.4 %copy-start.18 = (s32[8]{0:T(128)S(1)}, s32[8]{0:T(128)}, u32[]{:S(2)}) copy-start(s32[8]{0:T(128)} %counts_ref.1) | copy-start | bytes 100
  12.0 13.4 %collective-permute-start.6 = (bf16[256,384]{1,0:T(8,128)(2,1)S(1)}, bf16[256,384]{1,0:T(8,128)(2,1)S(1)}, u32[]{:S(2)}, u32[]{:S(2)}) collective-permute-start(bf16[256,384]{1,0:T(8,128)(2,1)S(1)} %get-tuple-element.25), channel_id=1, source_target_pairs={{0,28},{4,24},{8,20},{12,16},{16,12},{20,8},{24,4},{28,0},{1,29},{... | collective-permute-start | bytes 589832 | tf_op jit(solution)/shard_map/ppermute | solution.py:307
  46.7 0.6 copy-start.2
  47.3 48.9 %collective-permute-start.10 = (bf16[272,128]{1,0:T(8,128)(2,1)S(1)}, bf16[272,128]{1,0:T(8,128)(2,1)S(1)}, u32[]{:S(2)}, u32[]{:S(2)}) collective-permute-start(bf16[272,128]{1,0:T(8,128)(2,1)S(1)} %get-tuple-element.30), channel_id=1, source_target_pairs={{0,16},{4,20},{8,24},{12,28},{16,0},{20,4},{24,8},{28,12},{1,17},{... | collective-permute-start | bytes 208904 | tf_op jit(solution)/shard_map/ppermute | solution.py:307
  49.2 48.7 %collective-permute-start.11 = (bf16[272,128]{1,0:T(8,128)(2,1)S(1)}, bf16[272,128]{1,0:T(8,128)(2,1)S(1)}, u32[]{:S(2)}, u32[]{:S(2)}) collective-permute-start(bf16[272,128]{1,0:T(8,128)(2,1)S(1)} %get-tuple-element.31), channel_id=1, source_target_pairs={{0,20},{4,16},{8,28},{12,24},{16,4},{20,0},{24,12},{28,8},{1,21},{... | collective-permute-start | bytes 208904 | tf_op jit(solution)/shard_map/ppermute | solution.py:307
  49.3 48.7 %collective-permute-start.12 = (bf16[272,128]{1,0:T(8,128)(2,1)S(1)}, bf16[272,128]{1,0:T(8,128)(2,1)S(1)}, u32[]{:S(2)}, u32[]{:S(2)}) collective-permute-start(bf16[272,128]{1,0:T(8,128)(2,1)S(1)} %get-tuple-element.32), channel_id=1, source_target_pairs={{0,24},{4,28},{8,16},{12,20},{16,8},{20,12},{24,0},{28,4},{1,25},{... | collective-permute-start | bytes 208904 | tf_op jit(solution)/shard_map/ppermute | solution.py:307
  94.3 4.6 %collective-permute-start.13 = (bf16[272,128]{1,0:T(8,128)(2,1)S(1)}, bf16[272,128]{1,0:T(8,128)(2,1)S(1)}, u32[]{:S(2)}, u32[]{:S(2)}) collective-permute-start(bf16[272,128]{1,0:T(8,128)(2,1)S(1)} %get-tuple-element.33), channel_id=1, source_target_pairs={{0,28},{4,24},{8,20},{12,16},{16,12},{20,8},{24,4},{28,0},{1,29},{... | collective-permute-start | bytes 208904 | tf_op jit(solution)/shard_map/ppermute | solution.py:307
  96.1 2.9 %collective-permute-start.7 = (bf16[272,128]{1,0:T(8,128)(2,1)S(1)}, bf16[272,128]{1,0:T(8,128)(2,1)S(1)}, u32[]{:S(2)}, u32[]{:S(2)}) collective-permute-start(bf16[272,128]{1,0:T(8,128)(2,1)S(1)} %get-tuple-element.27), channel_id=1, source_target_pairs={{0,4},{4,0},{8,12},{12,8},{16,20},{20,16},{24,28},{28,24},{1,5},{5... | collective-permute-start | bytes 208904 | tf_op jit(solution)/shard_map/ppermute | solution.py:307
  96.2 6.3 %copy-start.4 = (bf16[272,128]{1,0:T(8,128)(2,1)}, bf16[272,128]{1,0:T(8,128)(2,1)S(1)}, u32[]{:S(2)}) copy-start(bf16[272,128]{1,0:T(8,128)(2,1)S(1)} %collective-permute-done.10.refs_4_) | copy-start | bytes 208900
  96.2 5.6 %collective-permute-start.8 = (bf16[272,128]{1,0:T(8,128)(2,1)S(1)}, bf16[272,128]{1,0:T(8,128)(2,1)S(1)}, u32[]{:S(2)}, u32[]{:S(2)}) collective-permute-start(bf16[272,128]{1,0:T(8,128)(2,1)S(1)} %get-tuple-element.28), channel_id=1, source_target_pairs={{0,8},{4,12},{8,0},{12,4},{16,24},{20,28},{24,16},{28,20},{1,9},{5... | collective-permute-start | bytes 208904 | tf_op jit(solution)/shard_map/ppermute | solution.py:307
  97.9 4.6 %copy-start.6 = (bf16[272,128]{1,0:T(8,128)(2,1)}, bf16[272,128]{1,0:T(8,128)(2,1)S(1)}, u32[]{:S(2)}) copy-start(bf16[272,128]{1,0:T(8,128)(2,1)S(1)} %collective-permute-done.11.refs_5_) | copy-start | bytes 208900
  98.0 4.6 %collective-permute-start.9 = (bf16[272,128]{1,0:T(8,128)(2,1)S(1)}, bf16[272,128]{1,0:T(8,128)(2,1)S(1)}, u32[]{:S(2)}, u32[]{:S(2)}) collective-permute-start(bf16[272,128]{1,0:T(8,128)(2,1)S(1)} %get-tuple-element.29), channel_id=1, source_target_pairs={{0,12},{4,8},{8,4},{12,0},{16,28},{20,24},{24,20},{28,16},{1,13},{... | collective-permute-start | bytes 208904 | tf_op jit(solution)/shard_map/ppermute | solution.py:307
  98.0 4.5 %copy-start.8 = (bf16[272,128]{1,0:T(8,128)(2,1)}, bf16[272,128]{1,0:T(8,128)(2,1)S(1)}, u32[]{:S(2)}) copy-start(bf16[272,128]{1,0:T(8,128)(2,1)S(1)} %collective-permute-done.12.refs_6_) | copy-start | bytes 208900
  99.0 3.6 %copy-start.10 = (bf16[272,128]{1,0:T(8,128)(2,1)}, bf16[272,128]{1,0:T(8,128)(2,1)S(1)}, u32[]{:S(2)}) copy-start(bf16[272,128]{1,0:T(8,128)(2,1)S(1)} %collective-permute-done.13.refs_7_) | copy-start | bytes 208900
  99.0 3.6 %copy-start.12 = (bf16[272,128]{1,0:T(8,128)(2,1)}, bf16[272,128]{1,0:T(8,128)(2,1)S(1)}, u32[]{:S(2)}) copy-start(bf16[272,128]{1,0:T(8,128)(2,1)S(1)} %collective-permute-done.7.refs_1_) | copy-start | bytes 208900
  101.8 0.7 copy-start.14
  102.5 0.6 copy-start.16
  103.1 7.0 %copy-start.3 = (bf16[272,128]{1,0:T(8,128)(2,1)S(1)}, bf16[272,128]{1,0:T(8,128)(2,1)}, u32[]{:S(2)}) copy-start(bf16[272,128]{1,0:T(8,128)(2,1)} %copy-done.2) | copy-start | bytes 208900
  104.5 13.0 %collective-permute-start.14 = (f32[1,128]{1,0:T(1,128)}, f32[1,128]{1,0:T(1,128)S(1)}, u32[]{:S(2)}, u32[]{:S(2)}) collective-permute-start(f32[1,128]{1,0:T(1,128)} %sum_kl.1), channel_id=1, source_target_pairs={{0,1},{1,0},{2,3},{3,2},{4,5},{5,4},{6,7},{7,6},{8,9},{9,8},{10,11... | collective-permute-start | bytes 1544 | tf_op jit(solution)/shard_map/ppermute | solution.py:351
  104.5 13.0 %collective-permute-start.15 = (f32[1,128]{1,0:T(1,128)}, f32[1,128]{1,0:T(1,128)S(1)}, u32[]{:S(2)}, u32[]{:S(2)}) collective-permute-start(f32[1,128]{1,0:T(1,128)} %sum_kl.1), channel_id=1, source_target_pairs={{0,2},{1,3},{2,0},{3,1},{4,6},{5,7},{6,4},{7,5},{8,10},{9,11},{10,... | collective-permute-start | bytes 1544 | tf_op jit(solution)/shard_map/ppermute | solution.py:351
  104.5 13.0 %collective-permute-start.16 = (f32[1,128]{1,0:T(1,128)}, f32[1,128]{1,0:T(1,128)S(1)}, u32[]{:S(2)}, u32[]{:S(2)}) collective-permute-start(f32[1,128]{1,0:T(1,128)} %sum_kl.1), channel_id=1, source_target_pairs={{0,3},{1,2},{2,1},{3,0},{4,7},{5,6},{6,5},{7,4},{8,11},{9,10},{10,... | collective-permute-start | bytes 1544 | tf_op jit(solution)/shard_map/ppermute | solution.py:351
  110.2 0.9 copy-start.5
  111.0 0.9 copy-start.7
  111.9 0.9 copy-start.9
  112.8 0.9 copy-start.11
  113.7 0.9 copy-start.13
  114.6 0.9 copy-start.15
  115.5 0.9 copy-start.17
  116.3 1.1 copy-start.19

commit v4 on v3

--- a/solution.py
+++ b/solution.py
@@ -45,20 +45,61 @@
             pl.when(index == part)(functools.partial(act, pl.ds(part * width, width)))
 
 
-def pack_kernel(blocks, me_ref, teacher_ref, student_ref, *sends):
+def pack_folded_kernel(blocks, chunks, me_ref, teacher_ref, student_ref, *refs):
+    sends, student, sems = refs[: 2 * chunks], refs[2 * chunks], refs[2 * chunks + 1]
+    rows = teacher_ref.shape[0]
+    half = rows // 2
+    copies = [pltpu.make_async_copy(student_ref, student, sems.at[2 * chunks * blocks // 2])]
+    for chunk in range(chunks):
+        for core in range(2):
+            for k in range(blocks // 2):
+                to = jnp.bitwise_xor(me_ref[0], 2 * k + core)
+                at = pl.multiple_of((to * chunks + chunk) * LANES, LANES)
+                copies.append(
+                    pltpu.make_async_copy(
+                        teacher_ref.at[:, pl.ds(at, LANES)],
+                        sends[2 * chunk + core].at[k, pl.ds(0, rows)],
+                        sems.at[(2 * chunk + core) * (blocks // 2) + k],
+                    )
+                )
+    for copy in copies:
+        copy.start()
+    copies[0].wait()
+    for core in range(2):
+        for k in range(blocks // 2):
+            to = jnp.bitwise_xor(me_ref[0], 2 * k + core)
+            lanes = pl.ds(pl.multiple_of(to * LANES, LANES), LANES)
+            top, bottom = student[:half, lanes], student[half:, lanes]
+            for chunk in range(chunks):
+                part = slice(chunk * (LANES // 2), (chunk + 1) * (LANES // 2))
+                sends[2 * chunk + core][k, rows:, :] = jnp.concatenate(
+                    [top[:, part], bottom[:, part]], axis=1
+                )
+    for copy in copies[1:]:
+        copy.wait()
+
+
+def pack_plain_kernel(blocks, me_ref, teacher_ref, student_ref, *sends):
     teacher_width = teacher_ref.shape[1] // blocks
     student_width = student_ref.shape[1] // blocks
-    for k in range(blocks):
-        to = jnp.bitwise_xor(me_ref[0], k)
-
-        def put_teacher(columns, send=sends[k]):
-            send[:, :teacher_width] = teacher_ref[:, columns]
-
-        def put_student(columns, send=sends[k]):
-            send[:, teacher_width:] = student_ref[:, columns]
-
-        at_columns(to, blocks, teacher_width, put_teacher)
-        at_columns(to, blocks, student_width, put_student)
+    for core in range(2):
+        for k in range(blocks // 2):
+            to = jnp.bitwise_xor(me_ref[0], 2 * k + core)
+
+            def put_teacher(columns, send=sends[core], k=k):
+                send[k, :, :teacher_width] = teacher_ref[:, columns]
+
+            def put_student(columns, send=sends[core], k=k):
+                send[k, :, teacher_width:] = student_ref[:, columns]
+
+            at_columns(to, blocks, teacher_width, put_teacher)
+            at_columns(to, blocks, student_width, put_student)
+
+
+def merge_kernel(kept_ref, swapped_ref, *sends):
+    for k, send in enumerate(sends):
+        send[0] = kept_ref[k + 1]
+        send[1] = swapped_ref[k + 1]
 
 
 def pair_sum(parts):
@@ -67,19 +108,26 @@
     return parts[0]
 
 
-def sum_kernel(*refs):
-    total = pair_sum([ref[...].astype(jnp.float32) for ref in refs[:-1]])
-    refs[-1][...] = jnp.sum(total, axis=0, keepdims=True)
-
-
-def unpack_kernel(blocks, me_ref, *refs):
-    grad_ref = refs[blocks]
-    for k in range(blocks):
-
-        def put(columns, source=refs[k]):
-            grad_ref[:, columns] = source[: grad_ref.shape[0], :].astype(jnp.float32)
-
-        at_columns(jnp.bitwise_xor(me_ref[0], k), blocks, refs[k].shape[1], put)
+def arrived(refs):
+    return [refs[0].at[0], refs[1].at[0]] + [ref.at[core] for ref in refs[2:] for core in range(2)]
+
+
+def sum_kernel(counts_ref, *refs):
+    blocks = arrived(refs[:-1])
+    total = pair_sum([block[block.shape[0] - TAIL :, :].astype(jnp.float32) for block in blocks])
+    tokens = sum(counts_ref[b] for b in range(len(blocks)))
+    refs[-1][...] = jnp.sum(total, axis=0, keepdims=True) / (H_REL * tokens).astype(jnp.float32)
+
+
+def unpack_kernel(me_ref, *refs):
+    grad_ref = refs[-1]
+    blocks = arrived(refs[:-1])
+    for k, block in enumerate(blocks):
+
+        def put(columns, block=block):
+            grad_ref[:, columns] = block[: grad_ref.shape[0], :].astype(jnp.float32)
+
+        at_columns(jnp.bitwise_xor(me_ref[0], k), len(blocks), block.shape[1], put)
 
 
 def fold(values):
@@ -87,25 +135,24 @@
     return jnp.sum(values.reshape(rows // 8, 8, columns), axis=0)
 
 
-def relation_kernel(blocks, heads, tiles, me_ref, counts_ref, *refs):
-    sources = refs[:blocks]
-    grads = refs[blocks : 2 * blocks]
-    (
-        pack,
-        key_op,
-        row_op,
-        student_col,
-        teacher_prob,
-        student_prob,
-        grad_cols,
-        grad_rows,
-        kl_sum,
-    ) = refs[2 * blocks :]
+def relation_kernel(folded, heads, tiles, n_in, n_done, last, me_ref, counts_ref, *refs):
+    sources = arrived(refs[:n_in])
+    done = refs[n_in : n_in + 2 * n_done]
+    out_a, out_b, pack, key_op, row_op, student_col, teacher_prob, student_prob = refs[
+        n_in + 2 * n_done : n_in + 2 * n_done + 8
+    ]
+    if last:
+        grad_cols, kl_sum, grad_rows = refs[n_in + 2 * n_done + 8 :]
+    else:
+        grad_cols, kl_sum = out_a, out_b
     f32, bf16 = jnp.float32, jnp.bfloat16
-    rows = sources[0].shape[0]
+    blocks = len(sources)
+    rows = teacher_prob.shape[1]
+    half = rows // 2
     live = tiles * rows
     window = rows + PAD
     student_at = heads * TEACHER_DIM
+    student_width = heads * STUDENT_DIM
     filled = 2 * TEACHER_DIM + 2 * STUDENT_DIM
 
     position = lax.broadcasted_iota(jnp.int32, (window, rows), 0)
@@ -119,8 +166,18 @@
         places.append((base, start - base, counts_ref[owner]))
     for source, (base, shift, count) in zip(sources, places):
         place = ((position == token + shift) & (token < count)).astype(bf16)
-        moved = jnp.dot(place, source[...], preferred_element_type=f32)
-        pack[pl.ds(base, window), :] = pack[pl.ds(base, window), :] + moved
+        here = pl.ds(base, window)
+        if folded:
+            moved = jnp.dot(place, source[:rows, :], preferred_element_type=f32)
+            pack[here, :student_at] = pack[here, :student_at] + moved
+            student = source[rows:, :]
+            moved = jnp.dot(
+                place[:, :half], student[:, :student_width], preferred_element_type=f32
+            ) + jnp.dot(place[:, half:], student[:, student_width:], preferred_element_type=f32)
+            pack[here, student_at:] = pack[here, student_at:] + moved
+        else:
+            moved = jnp.dot(place, source[...], preferred_element_type=f32)
+            pack[here, :] = pack[here, :] + moved
 
     ones = jnp.ones((rows, DEPTH - filled), bf16)
     spare = lax.broadcasted_iota(jnp.int32, (DEPTH - filled, rows), 0)
@@ -267,85 +324,145 @@
 
         lax.fori_loop(0, heads * tiles, row_step, 0)
 
+    if not last:
+        return
+
+    parts = [ref for ref in done[::2]] + [grad_cols]
+    total_width = len(parts) * student_width
     for i in range(tiles):
-        columns = grad_cols[:, i].reshape(heads * STUDENT_DIM, rows)
+        columns = jnp.concatenate([p[:, i].reshape(student_width, rows) for p in parts], axis=0)
         grad_rows[pl.ds(i * rows, rows), :] = columns.T * (STUDENT_DIM**-0.5)
-    grad_rows[pl.ds(live, window), :] = jnp.zeros((window, heads * STUDENT_DIM), f32)
-    divergence = jnp.sum(kl_sum[...], axis=1, keepdims=True) * math.log(2.0)
-    parts = [part.astype(f32) for part in split_three(divergence)]
-    line = lax.broadcasted_iota(jnp.int32, (TAIL, heads * STUDENT_DIM), 0)
-    tail = jnp.where(line == 0, parts[0], 0.0)
-    tail = jnp.where(line == 1, parts[1], tail)
-    tail = jnp.where(line == 2, parts[2], tail).astype(bf16)
+    grad_rows[pl.ds(live, window), :] = jnp.zeros((window, total_width), f32)
+    kl_total = sum([ref[...] for ref in done[1::2]] + [kl_sum[...]])
+    divergence = jnp.sum(kl_total, axis=1, keepdims=True) * math.log(2.0)
+    thirds = [part.astype(f32) for part in split_three(divergence)]
+    line = lax.broadcasted_iota(jnp.int32, (TAIL, total_width), 0)
+    tail = jnp.where(line == 0, thirds[0], 0.0)
+    tail = jnp.where(line == 1, thirds[1], tail)
+    tail = jnp.where(line == 2, thirds[2], tail).astype(bf16)
     position = lax.broadcasted_iota(jnp.int32, (rows, window), 1)
     token = lax.broadcasted_iota(jnp.int32, (rows, window), 0)
-    for grad, (base, shift, count) in zip(grads, places):
+    for k, (base, shift, count) in enumerate(places):
+        out = out_b if k % 2 else out_a
         place = ((position == token + shift) & (token < count)).astype(bf16)
         block = grad_rows[pl.ds(base, window), :].astype(bf16)
-        grad[:rows, :] = jnp.dot(place, block, preferred_element_type=f32).astype(bf16)
-        grad[rows:, :] = tail
+        out[k // 2, :rows, :] = jnp.dot(place, block, preferred_element_type=f32).astype(bf16)
+        out[k // 2, rows:, :] = tail
 
 
 def local(teacher_queries, student_queries, token_counts):
     f32, bf16 = jnp.float32, jnp.bfloat16
     blocks = lax.axis_size("seq")
+    chips = blocks // 2
+    groups = lax.axis_size("head")
     rows = teacher_queries.shape[0]
     heads = teacher_queries.shape[1] // TEACHER_DIM // blocks
     tiles = blocks * 3 // 4
     live = tiles * rows
-    width = heads * (TEACHER_DIM + STUDENT_DIM)
+    folded = heads * STUDENT_DIM == LANES
+    chunks = 2 if folded else 1
+    chunk_heads = heads // chunks
+    teacher_width = chunk_heads * TEACHER_DIM
+    student_width = chunk_heads * STUDENT_DIM
+    if folded:
+        send_shape = (chips, rows + rows // 2, LANES)
+    else:
+        send_shape = (chips, rows, teacher_width + student_width)
     vmem = pl.BlockSpec(memory_space=pltpu.VMEM)
     smem = pl.BlockSpec(memory_space=pltpu.SMEM)
-    params = pltpu.CompilerParams(vmem_limit_bytes=48 * 1024 * 1024)
+    params = pltpu.CompilerParams(vmem_limit_bytes=40 * 1024 * 1024)
     me = lax.axis_index("seq").reshape(1)
-
-    far_first = sorted(range(1, blocks), key=lambda k: -(k >> 1).bit_count())
-
-    def exchange(sends):
-        out = list(sends)
+    far_first = sorted(range(1, chips), key=lambda k: -k.bit_count())
+
+    def exchange(kept, swapped):
+        swapped = lax.ppermute(swapped, "seq", [(i, i ^ 1) for i in range(blocks)])
+        shape = (2,) + kept.shape[1:]
+        sends = pl.pallas_call(
+            merge_kernel,
+            in_specs=[vmem] * 2,
+            out_specs=[vmem] * (chips - 1),
+            out_shape=[jax.ShapeDtypeStruct(shape, bf16)] * (chips - 1),
+            compiler_params=params,
+            name="merge",
+        )(kept, swapped)
+        out = [None] * (chips - 1)
         for k in far_first:
-            out[k] = lax.ppermute(sends[k], "seq", [(i, i ^ k) for i in range(blocks)])
-        return out
-
-    sends = pl.pallas_call(
-        functools.partial(pack_kernel, blocks),
-        in_specs=[smem, vmem, vmem],
-        out_specs=[vmem] * blocks,
-        out_shape=[jax.ShapeDtypeStruct((rows, width), bf16)] * blocks,
-        compiler_params=params,
-        name="pack",
-    )(me, teacher_queries, student_queries)
-    sources = exchange(sends)
-    grads = pl.pallas_call(
-        functools.partial(relation_kernel, blocks, heads, tiles),
-        in_specs=[smem, smem] + [vmem] * blocks,
-        out_specs=[vmem] * blocks,
-        out_shape=[jax.ShapeDtypeStruct((rows + TAIL, heads * STUDENT_DIM), bf16)] * blocks,
-        scratch_shapes=[
-            pltpu.VMEM((live + rows + PAD, width), f32),
-            pltpu.VMEM((heads, live, DEPTH), bf16),
-            pltpu.VMEM((heads, tiles, DEPTH, 2 * rows), bf16),
-            pltpu.VMEM((heads, tiles, STUDENT_DIM, rows), bf16),
+            pairs = [(i, i ^ (2 * k)) for i in range(blocks)]
+            out[k - 1] = lax.ppermute(sends[k - 1], "seq", pairs)
+        return [kept, swapped] + out
+
+    packed = jax.ShapeDtypeStruct(send_shape, bf16)
+    if folded:
+        anywhere = pl.BlockSpec(memory_space=pl.ANY)
+        sends = pl.pallas_call(
+            functools.partial(pack_folded_kernel, blocks, chunks),
+            in_specs=[smem, anywhere, anywhere],
+            out_specs=[vmem] * (2 * chunks),
+            out_shape=[packed] * (2 * chunks),
+            scratch_shapes=[
+                pltpu.VMEM(student_queries.shape, bf16),
+                pltpu.SemaphoreType.DMA((chunks * blocks + 1,)),
+            ],
+            compiler_params=params,
+            name="pack",
+        )(me, teacher_queries, student_queries)
+    else:
+        sends = pl.pallas_call(
+            functools.partial(pack_plain_kernel, blocks),
+            in_specs=[smem, vmem, vmem],
+            out_specs=[vmem] * 2,
+            out_shape=[packed] * 2,
+            compiler_params=params,
+            name="pack",
+        )(me, teacher_queries, student_queries)
+    incoming = [exchange(*sends[2 * c : 2 * c + 2]) for c in range(chunks)]
+
+    result = jax.ShapeDtypeStruct((chunk_heads, tiles, STUDENT_DIM, rows), f32)
+    message = jax.ShapeDtypeStruct((chips, rows + TAIL, heads * STUDENT_DIM), bf16)
+    kl_shape = jax.ShapeDtypeStruct((1, rows), f32)
+    pairs = chunk_heads * tiles * (tiles + 1) // 2 * rows * rows
+    done = []
+    for c in range(chunks):
+        last = c == chunks - 1
+        scratch = [
+            pltpu.VMEM((live + rows + PAD, teacher_width + student_width), f32),
+            pltpu.VMEM((chunk_heads, live, DEPTH), bf16),
+            pltpu.VMEM((chunk_heads, tiles, DEPTH, 2 * rows), bf16),
+            pltpu.VMEM((chunk_heads, tiles, STUDENT_DIM, rows), bf16),
             pltpu.VMEM((tiles, rows, rows), f32),
             pltpu.VMEM((tiles, rows, rows), f32),
-            pltpu.VMEM((heads, tiles, STUDENT_DIM, rows), f32),
-            pltpu.VMEM((live + rows + PAD, heads * STUDENT_DIM), f32),
-            pltpu.VMEM((1, rows), f32),
-        ],
-        compiler_params=params,
-        name="relation",
-    )(me, token_counts, *sources)
-    grads = exchange(grads)
+        ]
+        if last:
+            scratch += [
+                pltpu.VMEM(result.shape, f32),
+                pltpu.VMEM(kl_shape.shape, f32),
+                pltpu.VMEM((live + rows + PAD, heads * STUDENT_DIM), f32),
+            ]
+        inputs = [me, token_counts, *incoming[c], *done]
+        done += pl.pallas_call(
+            functools.partial(
+                relation_kernel, folded, chunk_heads, tiles, len(incoming[c]), c, last
+            ),
+            in_specs=[smem, smem] + [vmem] * (len(inputs) - 2),
+            out_specs=[vmem] * 2,
+            out_shape=[message, message] if last else [result, kl_shape],
+            scratch_shapes=scratch,
+            compiler_params=params,
+            cost_estimate=pl.CostEstimate(
+                flops=4 * pairs * DEPTH, bytes_accessed=8 * pairs, transcendentals=2 * pairs
+            ),
+            name="relation",
+        )(*inputs)
+    returned = exchange(*done[-2:])
     kl = pl.pallas_call(
         sum_kernel,
-        grid=(1,),
-        in_specs=[pl.BlockSpec((TAIL, heads * STUDENT_DIM), lambda _: (rows // TAIL, 0))] * blocks,
-        out_specs=pl.BlockSpec((1, heads * STUDENT_DIM), lambda _: (0, 0)),
+        in_specs=[smem] + [vmem] * len(returned),
+        out_specs=vmem,
         out_shape=jax.ShapeDtypeStruct((1, heads * STUDENT_DIM), f32),
+        compiler_params=params,
         name="sum_kl",
-    )(*grads)
-    groups = lax.axis_size("head")
-    total = pair_sum(
+    )(token_counts, *returned)
+    loss = pair_sum(
         [kl]
         + [
             lax.ppermute(kl, "head", [(i, i ^ k) for i in range(groups)])
@@ -353,14 +470,14 @@
         ]
     )
     grad = pl.pallas_call(
-        functools.partial(unpack_kernel, blocks),
-        in_specs=[smem] + [vmem] * blocks,
+        unpack_kernel,
+        in_specs=[smem] + [vmem] * len(returned),
         out_specs=vmem,
         out_shape=jax.ShapeDtypeStruct((rows, student_queries.shape[1]), f32),
         compiler_params=params,
         name="unpack",
-    )(me, *grads)
-    return (grad, total[0, 0] / (H_REL * jnp.sum(token_counts).astype(f32)))
+    )(me, *returned)
+    return (grad, loss[0, 0])
 
 
 def solution(mesh):

time: 120 us -> 84.7 us (0.71); the launches traced: 119 us -> 84.6 us
  starting transfers between devices: 64.3 us -> 39.5 us
  local copies, waits for them, and re-layouts: 9.66 us -> 2.26 us
  Pallas kernels: 24 us -> 26.3 us
  waiting for transfers between devices: 17.5 us -> 15.3 us
  between operations: 2.56 us -> 0.71 us
    ppermute x14 -> x12, starting transfers between devices: 59.9 us -> 15.2 us  [the longest x9 14.6 us: exchange(): out[k - 1] = lax.ppermute(sends[k - 1], 'seq', pairs)]
    ppermute x3, starting transfers between devices: 4.38 us -> 24.3 us  [local(): lax.ppermute(kl, 'head', [(i, i ^ k) for i in range(groups)])]
    unnamed x40 -> x6, local copies, waits for them, and re-layouts: 9.66 us -> 2.26 us
    ppermute x14 -> x12, waiting for transfers between devices: 17.5 us -> 12.9 us  [the longest x9 10.1 us: exchange(): out[k - 1] = lax.ppermute(sends[k - 1], 'seq', pairs)]
    ppermute x3, waiting for transfers between devices: 0.01 us -> 2.44 us  [local(): lax.ppermute(kl, 'head', [(i, i ^ k) for i in range(groups)])]
    pallas_call x4 -> x8, Pallas kernels: 24 us -> 26.3 us  [the longest x2 23.8 us: local(): pl.pallas_call(functools.partial(relation_kernel, folded, chunk_heads, ti...]
  transfers between devices with their start and end apart: 17 -> 15, of which waited for: 6 -> 9; matrix products, arithmetic and copies ran while one was open for 1% -> 0% of each run, Pallas kernels for 1% -> 15%
where the time goes in v4:
time: 84.7 us; the launch traced here: 84.6 us
  starting transfers between devices  39.5 us (47%)
  Pallas kernels  26.3 us (31%)
  waiting for transfers between devices  15.3 us (18%)
  local copies, waits for them, and re-layouts  2.26 us (3%)
    ppermute x3, starting transfers between devices, local(): lax.ppermute(kl, 'head', [(i, i ^ k) for i in range(groups)])  24.3 us
    pallas_call x2, Pallas kernels, local(): pl.pallas_call(functools.partial(relation_kernel, folded, chunk_heads, ti...  23.8 us
    ppermute x9, starting transfers between devices, exchange(): out[k - 1] = lax.ppermute(sends[k - 1], 'seq', pairs)  14.6 us
    ppermute x9, waiting for transfers between devices, exchange(): out[k - 1] = lax.ppermute(sends[k - 1], 'seq', pairs)  10.1 us
    ppermute x3, waiting for transfers between devices, exchange(): swapped = lax.ppermute(swapped, 'seq', [(i, i ^ 1) for i in range(blocks)])  2.82 us
    ppermute x3, waiting for transfers between devices, local(): lax.ppermute(kl, 'head', [(i, i ^ k) for i in range(groups)])  2.44 us
    unnamed x6, local copies, waits for them, and re-layouts  2.26 us
  transfers between devices with their start and end apart: 15, of which 9 were waited for; matrix products, arithmetic and copies ran while one was open for 0% of the time, Pallas kernels for 15%

profile of v4, /device:TPU:0, one launch (start us, length us, event | category | flops | bytes accessed | tf_op | source)
XLA Modules:
  0.0 84.6 jit_solution(3556410443292210777)
XLA Ops:
  0.6 0.0 copy-start
  0.6 1.2 %copy-done = bf16[256,2048]{1,0:T(8,128)(2,1)S(1)} copy-done((bf16[256,2048]{1,0:T(8,128)(2,1)S(1)}, bf16[256,2048]{1,0:T(8,128)(2,1)}, u32[]{:S(2)}) %copy-start) | copy-done | bytes 1048600
  1.9 0.0 copy-start.1
  1.9 1.0 %copy-done.1 = bf16[256,1024]{1,0:T(8,128)(2,1)S(1)} copy-done((bf16[256,1024]{1,0:T(8,128)(2,1)S(1)}, bf16[256,1024]{1,0:T(8,128)(2,1)}, u32[]{:S(2)}) %copy-start.1) | copy-done | bytes 524312
  2.9 0.7 pack.1
  3.6 0.5 collective-permute-start.4
  4.2 0.1 collective-permute-start
  4.2 1.3 %collective-permute-done.4.swapped_ref.refs_1_ = bf16[4,384,128]{2,1,0:T(8,128)(2,1)S(1)} collective-permute-done((bf16[4,384,128]{2,1,0:T(8,128)(2,1)S(1)}, bf16[4,384,128]{2,1,0:T(8,128)(2,1)S(1)}, u32[]{:S(2)}, u32[]{:S(2)}) %collective-permute-start.4) | collective-permute-done | bytes 393248 | tf_op jit(solution)/shard_map/ppermute | solution.py:378
  5.5 2.9 %collective-permute-start.5 = (bf16[2,384,128]{2,1,0:T(8,128)(2,1)S(1)}, bf16[2,384,128]{2,1,0:T(8,128)(2,1)S(1)}, u32[]{:S(2)}, u32[]{:S(2)}) collective-permute-start(bf16[2,384,128]{2,1,0:T(8,128)(2,1)S(1)} %get-tuple-element.26), channel_id=1, source_target_pairs={{0,8},{4,12},{8,0},{12,4},{16,24},{20,28},{24,16},{28,20},{1,9},{5... | collective-permute-start | bytes 589832 | tf_op jit(solution)/shard_map/ppermute | solution.py:391
  8.5 1.5 %collective-permute-start.6 = (bf16[2,384,128]{2,1,0:T(8,128)(2,1)S(1)}, bf16[2,384,128]{2,1,0:T(8,128)(2,1)S(1)}, u32[]{:S(2)}, u32[]{:S(2)}) collective-permute-start(bf16[2,384,128]{2,1,0:T(8,128)(2,1)S(1)} %get-tuple-element.27), channel_id=1, source_target_pairs={{0,16},{4,20},{8,24},{12,28},{16,0},{20,4},{24,8},{28,12},{1,17},{... | collective-permute-start | bytes 589832 | tf_op jit(solution)/shard_map/ppermute | solution.py:391
  10.0 0.0 collective-permute-start.7
  10.0 0.0 collective-permute-done.swapped_ref.refs_1_
  10.1 2.0 %collective-permute-start.1 = (bf16[2,384,128]{2,1,0:T(8,128)(2,1)S(1)}, bf16[2,384,128]{2,1,0:T(8,128)(2,1)S(1)}, u32[]{:S(2)}, u32[]{:S(2)}) collective-permute-start(bf16[2,384,128]{2,1,0:T(8,128)(2,1)S(1)} %get-tuple-element.21), channel_id=1, source_target_pairs={{0,8},{4,12},{8,0},{12,4},{16,24},{20,28},{24,16},{28,20},{1,9},{5... | collective-permute-start | bytes 589832 | tf_op jit(solution)/shard_map/ppermute | solution.py:391
  12.1 0.0 copy-start.2
  12.1 1.5 %collective-permute-start.2 = (bf16[2,384,128]{2,1,0:T(8,128)(2,1)S(1)}, bf16[2,384,128]{2,1,0:T(8,128)(2,1)S(1)}, u32[]{:S(2)}, u32[]{:S(2)}) collective-permute-start(bf16[2,384,128]{2,1,0:T(8,128)(2,1)S(1)} %get-tuple-element.22), channel_id=1, source_target_pairs={{0,16},{4,20},{8,24},{12,28},{16,0},{20,4},{24,8},{28,12},{1,17},{... | collective-permute-start | bytes 589832 | tf_op jit(solution)/shard_map/ppermute | solution.py:391
  13.6 0.6 collective-permute-done.5.refs_2_
  14.2 3.0 %collective-permute-start.3 = (bf16[2,384,128]{2,1,0:T(8,128)(2,1)S(1)}, bf16[2,384,128]{2,1,0:T(8,128)(2,1)S(1)}, u32[]{:S(2)}, u32[]{:S(2)}) collective-permute-start(bf16[2,384,128]{2,1,0:T(8,128)(2,1)S(1)} %get-tuple-element.23), channel_id=1, source_target_pairs={{0,24},{4,28},{8,16},{12,20},{16,8},{20,12},{24,0},{28,4},{1,25},{... | collective-permute-start | bytes 589832 | tf_op jit(solution)/shard_map/ppermute | solution.py:391
  17.2 3.3 %collective-permute-done.6.refs_3_ = bf16[2,384,128]{2,1,0:T(8,128)(2,1)S(1)} collective-permute-done((bf16[2,384,128]{2,1,0:T(8,128)(2,1)S(1)}, bf16[2,384,128]{2,1,0:T(8,128)(2,1)S(1)}, u32[]{:S(2)}, u32[]{:S(2)}) %collective-permute-start.6) | collective-permute-done | bytes 196640 | tf_op jit(solution)/shard_map/ppermute | solution.py:391
  20.5 0.0 collective-permute-done.7.refs_4_
  20.5 0.0 copy-done.2
  20.5 11.4 %relation.2 = (f32[2,6,32,256]{3,2,1,0:T(8,128)S(1)}, f32[1,256]{1,0:T(1,128)S(1)}) custom-call(s32[1]{0:T(128)} %bitcast.me_ref, s32[8]{0:T(128)S(1)} %copy-done.2, bf16[4,384,128]{2,1,0:T(8,128)(2,1)S(1)} %get-tuple-element.24.kept_ref.refs_0_, bf16[4,384,128]{2,1,0:T(8,128)(2,1)S(1)} %collective-permute-done.4.swapped_ref.refs_1_, ...), custom_call_target="tpu_custom_call" | custom-call | flops 2818572288 | bytes 22020096 | tf_op jit(solution)/shard_map/relation/pallas_call | solution.py:442
  31.9 0.0 collective-permute-done.1.refs_2_
  31.9 0.0 collective-permute-done.2.refs_3_
  31.9 0.0 collective-permute-done.3.refs_4_
  31.9 12.4 %relation.3 = (bf16[4,272,128]{2,1,0:T(8,128)(2,1)S(1)}, bf16[4,272,128]{2,1,0:T(8,128)(2,1)S(1)}) custom-call(s32[1]{0:T(128)} %bitcast.me_ref, s32[8]{0:T(128)S(1)} %copy-done.2, bf16[4,384,128]{2,1,0:T(8,128)(2,1)S(1)} %get-tuple-element.19.kept_ref.refs_0_, bf16[4,384,128]{2,1,0:T(8,128)(2,1)S(1)} %collective-permute-done.swapped_ref.refs_1_, ...), custom_call_target="tpu_custom_call" | custom-call | flops 2818572288 | bytes 22020096 | tf_op jit(solution)/shard_map/relation/pallas_call | solution.py:442
  44.4 0.1 collective-permute-start.8
  44.4 1.5 %collective-permute-done.8.swapped_ref.refs_1_ = bf16[4,272,128]{2,1,0:T(8,128)(2,1)S(1)} collective-permute-done((bf16[4,272,128]{2,1,0:T(8,128)(2,1)S(1)}, bf16[4,272,128]{2,1,0:T(8,128)(2,1)S(1)}, u32[]{:S(2)}, u32[]{:S(2)}) %collective-permute-start.8) | collective-permute-done | bytes 278560 | tf_op jit(solution)/shard_map/ppermute | solution.py:378
  46.0 1.1 %collective-permute-start.9 = (bf16[2,272,128]{2,1,0:T(8,128)(2,1)S(1)}, bf16[2,272,128]{2,1,0:T(8,128)(2,1)S(1)}, u32[]{:S(2)}, u32[]{:S(2)}) collective-permute-start(bf16[2,272,128]{2,1,0:T(8,128)(2,1)S(1)} %get-tuple-element.33), channel_id=1, source_target_pairs={{0,8},{4,12},{8,0},{12,4},{16,24},{20,28},{24,16},{28,20},{1,9},{5... | collective-permute-start | bytes 417800 | tf_op jit(solution)/shard_map/ppermute | solution.py:391
  47.1 1.1 %collective-permute-start.10 = (bf16[2,272,128]{2,1,0:T(8,128)(2,1)S(1)}, bf16[2,272,128]{2,1,0:T(8,128)(2,1)S(1)}, u32[]{:S(2)}, u32[]{:S(2)}) collective-permute-start(bf16[2,272,128]{2,1,0:T(8,128)(2,1)S(1)} %get-tuple-element.34), channel_id=1, source_target_pairs={{0,16},{4,20},{8,24},{12,28},{16,0},{20,4},{24,8},{28,12},{1,17},{... | collective-permute-start | bytes 417800 | tf_op jit(solution)/shard_map/ppermute | solution.py:391
  48.2 1.4 %collective-permute-start.11 = (bf16[2,272,128]{2,1,0:T(8,128)(2,1)S(1)}, bf16[2,272,128]{2,1,0:T(8,128)(2,1)S(1)}, u32[]{:S(2)}, u32[]{:S(2)}) collective-permute-start(bf16[2,272,128]{2,1,0:T(8,128)(2,1)S(1)} %get-tuple-element.35), channel_id=1, source_target_pairs={{0,24},{4,28},{8,16},{12,20},{16,8},{20,12},{24,0},{28,4},{1,25},{... | collective-permute-start | bytes 417800 | tf_op jit(solution)/shard_map/ppermute | solution.py:391
  49.6 3.0 %collective-permute-done.9.refs_2_ = bf16[2,272,128]{2,1,0:T(8,128)(2,1)S(1)} collective-permute-done((bf16[2,272,128]{2,1,0:T(8,128)(2,1)S(1)}, bf16[2,272,128]{2,1,0:T(8,128)(2,1)S(1)}, u32[]{:S(2)}, u32[]{:S(2)}) %collective-permute-start.9) | collective-permute-done | bytes 139296 | tf_op jit(solution)/shard_map/ppermute | solution.py:391
  52.6 1.5 %collective-permute-done.10.refs_3_ = bf16[2,272,128]{2,1,0:T(8,128)(2,1)S(1)} collective-permute-done((bf16[2,272,128]{2,1,0:T(8,128)(2,1)S(1)}, bf16[2,272,128]{2,1,0:T(8,128)(2,1)S(1)}, u32[]{:S(2)}, u32[]{:S(2)}) %collective-permute-start.10) | collective-permute-done | bytes 139296 | tf_op jit(solution)/shard_map/ppermute | solution.py:391
  54.1 1.6 %collective-permute-done.11.refs_4_ = bf16[2,272,128]{2,1,0:T(8,128)(2,1)S(1)} collective-permute-done((bf16[2,272,128]{2,1,0:T(8,128)(2,1)S(1)}, bf16[2,272,128]{2,1,0:T(8,128)(2,1)S(1)}, u32[]{:S(2)}, u32[]{:S(2)}) %collective-permute-start.11) | collective-permute-done | bytes 139296 | tf_op jit(solution)/shard_map/ppermute | solution.py:391
  55.7 0.6 sum_kl.1
  56.3 22.7 %collective-permute-start.14 = (f32[1,128]{1,0:T(1,128)S(1)}, f32[1,128]{1,0:T(1,128)S(1)}, u32[]{:S(2)}, u32[]{:S(2)}) collective-permute-start(f32[1,128]{1,0:T(1,128)S(1)} %sum_kl.1), channel_id=1, source_target_pairs={{0,3},{1,2},{2,1},{3,0},{4,7},{5,6},{6,5},{7,4},{8,11},{9,10},{10,... | collective-permute-start | bytes 1544 | tf_op jit(solution)/shard_map/ppermute | solution.py:468
  79.0 1.6 %collective-permute-start.13 = (f32[1,128]{1,0:T(1,128)S(1)}, f32[1,128]{1,0:T(1,128)S(1)}, u32[]{:S(2)}, u32[]{:S(2)}) collective-permute-start(f32[1,128]{1,0:T(1,128)S(1)} %sum_kl.1), channel_id=1, source_target_pairs={{0,2},{1,3},{2,0},{3,1},{4,6},{5,7},{6,4},{7,5},{8,10},{9,11},{10,... | collective-permute-start | bytes 1544 | tf_op jit(solution)/shard_map/ppermute | solution.py:468
  80.6 0.0 collective-permute-start.12
  80.6 1.1 %unpack.1 = f32[256,1024]{1,0:T(8,128)} custom-call(s32[1]{0:T(128)} %bitcast.me_ref, bf16[4,272,128]{2,1,0:T(8,128)(2,1)S(1)} %get-tuple-element.31.kept_ref.refs_0_, bf16[4,272,128]{2,1,0:T(8,128)(2,1)S(1)} %collective-permute-done.8.swapped_ref.refs_1_, bf16[2,272,128]{2,1,0:T(8,128)(2,1)S(1)} %collective-permute-done.9.refs_2_, ...), custom_call_target="tpu_custom_call" | custom-call | tf_op jit(solution)/shard_map/unpack/pallas_call | solution.py:472
  81.7 0.0 collective-permute-done.14
  81.7 1.8 %collective-permute-done.13 = f32[1,128]{1,0:T(1,128)S(1)} collective-permute-done((f32[1,128]{1,0:T(1,128)S(1)}, f32[1,128]{1,0:T(1,128)S(1)}, u32[]{:S(2)}, u32[]{:S(2)}) %collective-permute-start.13) | collective-permute-done | bytes 544 | tf_op jit(solution)/shard_map/ppermute | solution.py:468
  83.4 0.7 collective-permute-done.12
  84.1 0.5 add_add_fusion
  (3 shorter events, 0.1 us)
Async XLA Ops:
  0.6 1.2 %copy-start = (bf16[256,2048]{1,0:T(8,128)(2,1)S(1)}, bf16[256,2048]{1,0:T(8,128)(2,1)}, u32[]{:S(2)}) copy-start(bf16[256,2048]{1,0:T(8,128)(2,1)} %teacher_ref.1) | copy-start | bytes 3145732
  1.9 1.0 %copy-start.1 = (bf16[256,1024]{1,0:T(8,128)(2,1)S(1)}, bf16[256,1024]{1,0:T(8,128)(2,1)}, u32[]{:S(2)}) copy-start(bf16[256,1024]{1,0:T(8,128)(2,1)} %student_ref.1) | copy-start | bytes 1572868
  3.6 1.9 %collective-permute-start.4 = (bf16[4,384,128]{2,1,0:T(8,128)(2,1)S(1)}, bf16[4,384,128]{2,1,0:T(8,128)(2,1)S(1)}, u32[]{:S(2)}, u32[]{:S(2)}) collective-permute-start(bf16[4,384,128]{2,1,0:T(8,128)(2,1)S(1)} %get-tuple-element.25), channel_id=1, source_target_pairs={{0,4},{4,0},{8,12},{12,8},{16,20},{20,16},{24,28},{28,24},{1,5},{5... | collective-permute-start | bytes 1179656 | tf_op jit(solution)/shard_map/ppermute | solution.py:378
  4.2 5.9 %collective-permute-start = (bf16[4,384,128]{2,1,0:T(8,128)(2,1)S(1)}, bf16[4,384,128]{2,1,0:T(8,128)(2,1)S(1)}, u32[]{:S(2)}, u32[]{:S(2)}) collective-permute-start(bf16[4,384,128]{2,1,0:T(8,128)(2,1)S(1)} %get-tuple-element.20), channel_id=1, source_target_pairs={{0,4},{4,0},{8,12},{12,8},{16,20},{20,16},{24,28},{28,24},{1,5},{5... | collective-permute-start | bytes 1179656 | tf_op jit(solution)/shard_map/ppermute | solution.py:378
  5.5 8.6 %collective-permute-start.5 = (bf16[2,384,128]{2,1,0:T(8,128)(2,1)S(1)}, bf16[2,384,128]{2,1,0:T(8,128)(2,1)S(1)}, u32[]{:S(2)}, u32[]{:S(2)}) collective-permute-start(bf16[2,384,128]{2,1,0:T(8,128)(2,1)S(1)} %get-tuple-element.26), channel_id=1, source_target_pairs={{0,8},{4,12},{8,0},{12,4},{16,24},{20,28},{24,16},{28,20},{1,9},{5... | collective-permute-start | bytes 589832 | tf_op jit(solution)/shard_map/ppermute | solution.py:391
  8.5 12.0 %collective-permute-start.6 = (bf16[2,384,128]{2,1,0:T(8,128)(2,1)S(1)}, bf16[2,384,128]{2,1,0:T(8,128)(2,1)S(1)}, u32[]{:S(2)}, u32[]{:S(2)}) collective-permute-start(bf16[2,384,128]{2,1,0:T(8,128)(2,1)S(1)} %get-tuple-element.27), channel_id=1, source_target_pairs={{0,16},{4,20},{8,24},{12,28},{16,0},{20,4},{24,8},{28,12},{1,17},{... | collective-permute-start | bytes 589832 | tf_op jit(solution)/shard_map/ppermute | solution.py:391
  10.0 10.5 %collective-permute-start.7 = (bf16[2,384,128]{2,1,0:T(8,128)(2,1)S(1)}, bf16[2,384,128]{2,1,0:T(8,128)(2,1)S(1)}, u32[]{:S(2)}, u32[]{:S(2)}) collective-permute-start(bf16[2,384,128]{2,1,0:T(8,128)(2,1)S(1)} %get-tuple-element.28), channel_id=1, source_target_pairs={{0,24},{4,28},{8,16},{12,20},{16,8},{20,12},{24,0},{28,4},{1,25},{... | collective-permute-start | bytes 589832 | tf_op jit(solution)/shard_map/ppermute | solution.py:391
  10.1 21.8 %collective-permute-start.1 = (bf16[2,384,128]{2,1,0:T(8,128)(2,1)S(1)}, bf16[2,384,128]{2,1,0:T(8,128)(2,1)S(1)}, u32[]{:S(2)}, u32[]{:S(2)}) collective-permute-start(bf16[2,384,128]{2,1,0:T(8,128)(2,1)S(1)} %get-tuple-element.21), channel_id=1, source_target_pairs={{0,8},{4,12},{8,0},{12,4},{16,24},{20,28},{24,16},{28,20},{1,9},{5... | collective-permute-start | bytes 589832 | tf_op jit(solution)/shard_map/ppermute | solution.py:391
  12.1 8.4 %copy-start.2 = (s32[8]{0:T(128)S(1)}, s32[8]{0:T(128)}, u32[]{:S(2)}) copy-start(s32[8]{0:T(128)} %counts_ref.5) | copy-start | bytes 100
  12.1 19.8 %collective-permute-start.2 = (bf16[2,384,128]{2,1,0:T(8,128)(2,1)S(1)}, bf16[2,384,128]{2,1,0:T(8,128)(2,1)S(1)}, u32[]{:S(2)}, u32[]{:S(2)}) collective-permute-start(bf16[2,384,128]{2,1,0:T(8,128)(2,1)S(1)} %get-tuple-element.22), channel_id=1, source_target_pairs={{0,16},{4,20},{8,24},{12,28},{16,0},{20,4},{24,8},{28,12},{1,17},{... | collective-permute-start | bytes 589832 | tf_op jit(solution)/shard_map/ppermute | solution.py:391
  14.2 17.7 %collective-permute-start.3 = (bf16[2,384,128]{2,1,0:T(8,128)(2,1)S(1)}, bf16[2,384,128]{2,1,0:T(8,128)(2,1)S(1)}, u32[]{:S(2)}, u32[]{:S(2)}) collective-permute-start(bf16[2,384,128]{2,1,0:T(8,128)(2,1)S(1)} %get-tuple-element.23), channel_id=1, source_target_pairs={{0,24},{4,28},{8,16},{12,20},{16,8},{20,12},{24,0},{28,4},{1,25},{... | collective-permute-start | bytes 589832 | tf_op jit(solution)/shard_map/ppermute | solution.py:391
  44.4 1.6 %collective-permute-start.8 = (bf16[4,272,128]{2,1,0:T(8,128)(2,1)S(1)}, bf16[4,272,128]{2,1,0:T(8,128)(2,1)S(1)}, u32[]{:S(2)}, u32[]{:S(2)}) collective-permute-start(bf16[4,272,128]{2,1,0:T(8,128)(2,1)S(1)} %get-tuple-element.32), channel_id=1, source_target_pairs={{0,4},{4,0},{8,12},{12,8},{16,20},{20,16},{24,28},{28,24},{1,5},{5... | collective-permute-start | bytes 835592 | tf_op jit(solution)/shard_map/ppermute | solution.py:378
  46.0 6.6 %collective-permute-start.9 = (bf16[2,272,128]{2,1,0:T(8,128)(2,1)S(1)}, bf16[2,272,128]{2,1,0:T(8,128)(2,1)S(1)}, u32[]{:S(2)}, u32[]{:S(2)}) collective-permute-start(bf16[2,272,128]{2,1,0:T(8,128)(2,1)S(1)} %get-tuple-element.33), channel_id=1, source_target_pairs={{0,8},{4,12},{8,0},{12,4},{16,24},{20,28},{24,16},{28,20},{1,9},{5... | collective-permute-start | bytes 417800 | tf_op jit(solution)/shard_map/ppermute | solution.py:391
  47.1 7.1 %collective-permute-start.10 = (bf16[2,272,128]{2,1,0:T(8,128)(2,1)S(1)}, bf16[2,272,128]{2,1,0:T(8,128)(2,1)S(1)}, u32[]{:S(2)}, u32[]{:S(2)}) collective-permute-start(bf16[2,272,128]{2,1,0:T(8,128)(2,1)S(1)} %get-tuple-element.34), channel_id=1, source_target_pairs={{0,16},{4,20},{8,24},{12,28},{16,0},{20,4},{24,8},{28,12},{1,17},{... | collective-permute-start | bytes 417800 | tf_op jit(solution)/shard_map/ppermute | solution.py:391
  48.2 7.6 %collective-permute-start.11 = (bf16[2,272,128]{2,1,0:T(8,128)(2,1)S(1)}, bf16[2,272,128]{2,1,0:T(8,128)(2,1)S(1)}, u32[]{:S(2)}, u32[]{:S(2)}) collective-permute-start(bf16[2,272,128]{2,1,0:T(8,128)(2,1)S(1)} %get-tuple-element.35), channel_id=1, source_target_pairs={{0,24},{4,28},{8,16},{12,20},{16,8},{20,12},{24,0},{28,4},{1,25},{... | collective-permute-start | bytes 417800 | tf_op jit(solution)/shard_map/ppermute | solution.py:391
  56.3 25.4 %collective-permute-start.14 = (f32[1,128]{1,0:T(1,128)S(1)}, f32[1,128]{1,0:T(1,128)S(1)}, u32[]{:S(2)}, u32[]{:S(2)}) collective-permute-start(f32[1,128]{1,0:T(1,128)S(1)} %sum_kl.1), channel_id=1, source_target_pairs={{0,3},{1,2},{2,1},{3,0},{4,7},{5,6},{6,5},{7,4},{8,11},{9,10},{10,... | collective-permute-start | bytes 1544 | tf_op jit(solution)/shard_map/ppermute | solution.py:468
  79.0 4.4 %collective-permute-start.13 = (f32[1,128]{1,0:T(1,128)S(1)}, f32[1,128]{1,0:T(1,128)S(1)}, u32[]{:S(2)}, u32[]{:S(2)}) collective-permute-start(f32[1,128]{1,0:T(1,128)S(1)} %sum_kl.1), channel_id=1, source_target_pairs={{0,2},{1,3},{2,0},{3,1},{4,6},{5,7},{6,4},{7,5},{8,10},{9,11},{10,... | collective-permute-start | bytes 1544 | tf_op jit(solution)/shard_map/ppermute | solution.py:468
  80.6 3.5 %collective-permute-start.12 = (f32[1,128]{1,0:T(1,128)S(1)}, f32[1,128]{1,0:T(1,128)S(1)}, u32[]{:S(2)}, u32[]{:S(2)}) collective-permute-start(f32[1,128]{1,0:T(1,128)S(1)} %sum_kl.1), channel_id=1, source_target_pairs={{0,1},{1,0},{2,3},{3,2},{4,5},{5,4},{6,7},{7,6},{8,9},{9,8},{10,11... | collective-permute-start | bytes 1544 | tf_op jit(solution)/shard_map/ppermute | solution.py:468
